TPU v7x, 512 devices: a whole 4x8x8 slice. The times are simulated.
512 devices in a mesh: gx: 8 (over z_hi, core), gy: 8 (over y), gz: 8 (over z_lo, x).
Axes of the slice: x: 4, y: 8, z: 8 (z_hi: 4, z_lo: 2; z = z_hi * 2 + z_lo), core: 2. Of those that a mesh axis runs over, the one named last changes fastest.
Arguments:
- normed: bfloat16 [4096, 3072], P(('gx', 'gz'), 'gy'), may hold values from -6 to 6
- grad_out: bfloat16 [4096, 3072], P(('gx', 'gz'), 'gy'), may hold values from -0.75 to 0.75
- grad_qkv_out: bfloat16 [4096, 9216], P(('gx', 'gy'), 'gz'), may hold values from -0.75 to 0.75
- pre_act: bfloat16 [4096, 12288], P(('gx', 'gy'), 'gz'), may hold values from -9 to 9
- w_qkv: bfloat16 [3072, 9216], P(('gy', 'gx'), 'gz'), may hold values from -0.109375 to 0.109375
- w_up: bfloat16 [3072, 12288], P(('gy', 'gx'), 'gz'), may hold values from -0.109375 to 0.109375
- w_down: bfloat16 [12288, 3072], P(('gz', 'gx'), 'gy'), may hold values from -0.0546875 to 0.0546875
Outputs:
- grad_input: bfloat16 [4096, 3072], P(('gx', 'gz'), 'gy')
- grad_w_qkv: bfloat16 [3072, 9216], P(('gy', 'gx'), 'gz')
- grad_w_up: bfloat16 [3072, 12288], P(('gy', 'gx'), 'gz')
- grad_w_down: bfloat16 [12288, 3072], P(('gz', 'gx'), 'gy')
All inputs are finite; a program needn't handle non-finite values.
Results may differ from a plain program's by a relative error of at most 0.028.
Values may be sent and summed in bfloat16 or wider, within the bound.
A program may use at most 64 MiB of HBM per device.

v0:
```python
import jax
import jax.numpy as jnp
from jax import lax
from jax.sharding import PartitionSpec as P


def gelu_parts(pre_act):
    pre_float = pre_act.astype(jnp.float32)
    normal_cdf = 0.5 * (1.0 + lax.erf(pre_float * 0.7071067811865476))
    normal_pdf = jnp.exp(-0.5 * pre_float * pre_float) * 0.3989422804014327
    return (pre_float * normal_cdf, normal_cdf + pre_float * normal_pdf)


def dot_rows(left, right):
    return lax.dot_general(
        left, right, (((1,), (1,)), ((), ())), preferred_element_type=jnp.float32
    )


def weight_term(left, right):
    return lax.dot_general(
        left, right, (((0,), (0,)), ((), ())), preferred_element_type=jnp.float32
    )


def shards(normed, grad_out, grad_qkv_out, pre_act, w_qkv, w_up, w_down):
    normed_rows, grad_rows = (
        lax.all_gather(normed, "gz", axis=0, tiled=True),
        lax.all_gather(grad_out, "gz", axis=0, tiled=True),
    )
    partial_act = dot_rows(grad_rows, lax.all_gather(w_down, "gx", axis=0, tiled=True))
    qkv_rows, pre_rows = (
        lax.all_gather(grad_qkv_out, "gy", axis=0, tiled=True),
        lax.all_gather(pre_act, "gy", axis=0, tiled=True),
    )
    grad_act = lax.psum(partial_act.astype(jnp.bfloat16), "gy").astype(jnp.float32)
    gelu_value, gelu_slope = gelu_parts(pre_rows)
    activated = gelu_value.astype(jnp.bfloat16)
    grad_pre = (grad_act * gelu_slope).astype(jnp.bfloat16)
    qkv_full, up_full = (
        lax.all_gather(w_qkv, "gx", axis=0, tiled=True),
        lax.all_gather(w_up, "gx", axis=0, tiled=True),
    )
    grad_input = lax.psum_scatter(
        (dot_rows(qkv_rows, qkv_full) + dot_rows(grad_pre, up_full)).astype(jnp.bfloat16),
        "gz",
        scatter_dimension=0,
        tiled=True,
    )
    grad_w_down = lax.psum_scatter(
        weight_term(activated, grad_rows).astype(jnp.bfloat16),
        "gx",
        scatter_dimension=0,
        tiled=True,
    )
    combined = jnp.concatenate((qkv_rows, grad_pre), axis=1)
    joined = lax.psum_scatter(
        weight_term(normed_rows, combined).astype(jnp.bfloat16),
        "gx",
        scatter_dimension=0,
        tiled=True,
    ).astype(jnp.float32)
    qkv_width = qkv_rows.shape[1]
    grad_w_qkv = joined[:, :qkv_width].astype(jnp.bfloat16)
    grad_w_up = joined[:, qkv_width:].astype(jnp.bfloat16)
    return (grad_input, grad_w_qkv, grad_w_up, grad_w_down)


def solution(mesh):
    placed = (
        P(("gx", "gz"), "gy"),
        P(("gx", "gz"), "gy"),
        P(("gx", "gy"), "gz"),
        P(("gx", "gy"), "gz"),
        P(("gy", "gx"), "gz"),
        P(("gy", "gx"), "gz"),
        P(("gz", "gx"), "gy"),
    )
    return jax.shard_map(
        shards,
        mesh=mesh,
        in_specs=placed,
        out_specs=(
            P(("gx", "gz"), "gy"),
            P(("gy", "gx"), "gz"),
            P(("gy", "gx"), "gz"),
            P(("gz", "gx"), "gy"),
        ),
        check_vma=False,
    )
```

profile of v0, /device:TPU:1, one launch (start us, length us, event | category | flops | bytes accessed | tf_op | source)
XLA Modules:
  0.0 400.4 jit_solution(9070100866324639032)
XLA Ops:
  7.2 0.7 all-gather.7.cloned.1.call-update
  7.9 0.7 all-gather.9.cloned.1.call-update
  8.7 24.7 %all_gather.23 = bf16[512,384]{1,0:T(8,128)(2,1)S(1)} all-gather(bf16[64,384]{1,0:T(8,128)(2,1)} %param.8), channel_id=1, replica_groups=mesh['gx'=8,'gy'=8,'gz'=8] {'gz'}, dimensions={0}, use_global_device_ids=true | all-gather | bytes 442368 | tf_op jit(solution)/shard_map/all_gather | solution.py:29
  33.4 16.5 %all-gather.7.cloned.1.call-done = bf16[1536,384]{1,0:T(8,128)(2,1)} async-done(((bf16[192,384]{1,0:T(8,128)(2,1)}), bf16[1536,384]{1,0:T(8,128)(2,1)}) %all-gather.7.cloned.1.call-update) | async-done | bytes 1179664 | tf_op jit(solution)/shard_map/all_gather | solution.py:31
  49.9 3.4 convolution_convert_fusion.1
  54.0 0.5 all-gather.11.cloned.1.call-update
  54.6 22.5 %all_gather.27 = bf16[512,384]{1,0:T(8,128)(2,1)S(1)} all-gather(bf16[64,384]{1,0:T(8,128)(2,1)S(1)} %copy-done.3), channel_id=1, replica_groups=mesh['gx'=8,'gy'=8,'gz'=8] {'gz'}, dimensions={0}, use_global_device_ids=true | all-gather | bytes 442368 | tf_op jit(solution)/shard_map/all_gather | solution.py:28
  77.1 11.9 %all-gather.9.cloned.1.call-done = bf16[512,1536]{1,0:T(8,128)(2,1)} async-done(((bf16[64,1536]{1,0:T(8,128)(2,1)}), bf16[512,1536]{1,0:T(8,128)(2,1)}) %all-gather.9.cloned.1.call-update) | async-done | bytes 1572880 | tf_op jit(solution)/shard_map/all_gather | solution.py:34
  89.0 85.8 %all-reduce.2.cloned.1.call-done = bf16[512,1536]{1,0:T(8,128)(2,1)} async-done(((bf16[512,1536]{1,0:T(8,128)(2,1)}), bf16[512,1536]{1,0:T(8,128)(2,1)}) %all-reduce.2.cloned.1.call-update) | async-done | bytes 1572880 | tf_op jit(solution)/shard_map/psum | solution.py:36
  174.8 3.8 fusion.8
  178.6 38.6 %all-gather.5.cloned.1.call-done = bf16[512,1152]{1,0:T(8,128)(2,1)} async-done(((bf16[64,1152]{1,0:T(8,128)(2,1)}), bf16[512,1152]{1,0:T(8,128)(2,1)}) %all-gather.5.cloned.1.call-update) | async-done | bytes 1179664 | tf_op jit(solution)/shard_map/all_gather | solution.py:33
  217.1 3.4 fusion
  220.5 2.5 copy.15
  223.1 0.8 copy-done.2
  223.9 26.1 %all_gather.22 = bf16[384,1152]{1,0:T(8,128)(2,1)S(1)} all-gather(bf16[48,1152]{1,0:T(8,128)(2,1)S(1)} %copy-done.2), channel_id=1, replica_groups=mesh['gx'=8,'gy'=8,'gz'=8] {'gx'}, dimensions={0}, use_global_device_ids=true | all-gather | bytes 995328 | tf_op jit(solution)/shard_map/all_gather | solution.py:41
  250.1 1.7 fusion.17
  251.8 6.1 %all-gather.11.cloned.1.call-done = bf16[384,1536]{1,0:T(8,128)(2,1)} async-done(((bf16[48,1536]{1,0:T(8,128)(2,1)}), bf16[384,1536]{1,0:T(8,128)(2,1)}) %all-gather.11.cloned.1.call-update) | async-done | bytes 1179664 | tf_op jit(solution)/shard_map/all_gather | solution.py:42
  257.9 3.2 fusion.14
  261.2 2.1 convolution_convert_fusion.2
  263.4 39.4 %reduce-scatter.10.cloned.1.call-done = bf16[48,2688]{1,0:T(8,128)(2,1)} async-done(((bf16[384,2688]{1,0:T(8,128)(2,1)}), bf16[48,2688]{1,0:T(8,128)(2,1)}) %reduce-scatter.10.cloned.1.call-update) | async-done | bytes 258064
  302.7 1.5 slice.10
  304.3 1.6 slice.11
  305.9 39.4 %reduce-scatter.6.cloned.1.call-done = bf16[64,384]{1,0:T(8,128)(2,1)} async-done(((bf16[512,384]{1,0:T(8,128)(2,1)}), bf16[64,384]{1,0:T(8,128)(2,1)}) %reduce-scatter.6.cloned.1.call-update) | async-done | bytes 49168 | tf_op jit(solution)/shard_map/reduce_scatter | solution.py:44
  345.2 48.4 %reduce-scatter.8.cloned.1.call-done = bf16[192,384]{1,0:T(8,128)(2,1)} async-done(((bf16[1536,384]{1,0:T(8,128)(2,1)}), bf16[192,384]{1,0:T(8,128)(2,1)}) %reduce-scatter.8.cloned.1.call-update) | async-done | bytes 147472 | tf_op jit(solution)/shard_map/reduce_scatter | solution.py:50
  (22 shorter events, 0.9 us)
Async XLA Ops:
  7.2 42.7 %all-gather.7.cloned.1.call-start = ((), (), s32[]{:S(2)}) async-start(), calls=%async_computation.4 | async-start | bytes 1327104 | tf_op jit(solution)/shard_map/all_gather | solution.py:31
  7.9 81.1 %all-gather.9.cloned.1.call-start = ((), (), s32[]{:S(2)}) async-start(), calls=%async_computation.6 | async-start | bytes 1769472 | tf_op jit(solution)/shard_map/all_gather | solution.py:34
  8.6 166.2 %all-reduce.2.cloned.1.call-start = ((), (), s32[]{:S(2)}) async-start(), calls=%async_computation.5 | async-start | bytes 3145728 | tf_op jit(solution)/shard_map/psum | solution.py:36
  33.4 21.2 %copy-start.3 = (bf16[64,384]{1,0:T(8,128)(2,1)S(1)}, bf16[64,384]{1,0:T(8,128)(2,1)}, u32[]{:S(2)}) copy-start(bf16[64,384]{1,0:T(8,128)(2,1)} %param.7) | copy-start | bytes 147460
  53.3 163.8 %all-gather.5.cloned.1.call-start = ((), (), s32[]{:S(2)}) async-start(), calls=%async_computation.3 | async-start | bytes 1327104 | tf_op jit(solution)/shard_map/all_gather | solution.py:33
  53.9 204.0 %all-gather.11.cloned.1.call-start = ((), (), s32[]{:S(2)}) async-start(), calls=%async_computation.7 | async-start | bytes 1327104 | tf_op jit(solution)/shard_map/all_gather | solution.py:42
  54.5 248.2 %reduce-scatter.10.cloned.1.call-start = ((), (), s32[]{:S(2)}) async-start(), calls=%async_computation.10 | async-start | bytes 2322432
  223.0 0.9 copy-start.2
  223.1 27.0 %copy-start.4 = (bf16[512,1152]{1,0:T(8,128)(2,1)S(1)}, bf16[512,1152]{1,0:T(8,128)(2,1)}, u32[]{:S(2)}) copy-start(bf16[512,1152]{1,0:T(8,128)(2,1)} %all-gather.5.cloned.1.call-done) | copy-start | bytes 3538948
  223.1 34.8 %copy-start.1 = (bf16[512,1536]{1,0:T(8,128)(2,1)S(1)}, bf16[512,1536]{1,0:T(8,128)(2,1)}, u32[]{:S(2)}) copy-start(bf16[512,1536]{1,0:T(8,128)(2,1)} %fusion.8) | copy-start | bytes 4718596
  223.1 122.1 %reduce-scatter.6.cloned.1.call-start = ((), (), s32[]{:S(2)}) async-start(), calls=%async_computation.8 | async-start | bytes 442368 | tf_op jit(solution)/shard_map/reduce_scatter | solution.py:44
  251.8 9.4 %copy-start = (bf16[512,1536]{1,0:T(8,128)(2,1)S(1)}, bf16[512,1536]{1,0:T(8,128)(2,1)}, u32[]{:S(2)}) copy-start(bf16[512,1536]{1,0:T(8,128)(2,1)} %all-gather.9.cloned.1.call-done) | copy-start | bytes 4718596
  261.2 132.4 %reduce-scatter.8.cloned.1.call-start = ((), (), s32[]{:S(2)}) async-start(), calls=%async_computation.9 | async-start | bytes 1327104 | tf_op jit(solution)/shard_map/reduce_scatter | solution.py:50
Sparse Core Ops, SparseCore 0:
  10.1 39.7 all-gather.6
  51.9 37.0 all-gather.8
  91.4 83.3 all-reduce.1
  176.8 40.3 all-gather.4
  219.1 38.7 all-gather.10
  260.6 42.0 reduce-scatter.9
  306.1 39.0 reduce-scatter.5
  348.9 44.7 reduce-scatter.7
where the time goes:
time: 402 us; the launch traced here: 400 us
  waiting for transfers between devices  288 us (72%)
  blocking collectives  73.4 us (18%)
  between operations  14.2 us (4%)
  matrix products  13.9 us (3%)
  local copies, waits for them, and re-layouts  6.48 us (2%)
    psum x1, waiting for transfers between devices, shards(): lax.psum(partial_act.astype(jnp.bfloat16), 'gy').astype(jnp.float32)  85.8 us
    reduce_scatter x1, waiting for transfers between devices, shards(): lax.psum_scatter(weight_term(activated, grad_rows).astype(jnp.bfloat16),...  48.4 us
    unnamed x9, waiting for transfers between devices  41.9 us
    reduce_scatter x1, waiting for transfers between devices, shards(): lax.psum_scatter((dot_rows(qkv_rows, qkv_full) + dot_rows(grad_pre, up_fu...  39.4 us
    all_gather x1, waiting for transfers between devices, shards(): lax.all_gather(grad_qkv_out, 'gy', axis=0, tiled=True)  38.6 us
    all_gather x1, blocking collectives, shards(): lax.all_gather(w_qkv, 'gx', axis=0, tiled=True)  26.1 us
    all_gather x1, blocking collectives, shards(): lax.all_gather(grad_out, 'gz', axis=0, tiled=True)  24.7 us
    all_gather x1, blocking collectives, shards(): lax.all_gather(normed, 'gz', axis=0, tiled=True)  22.5 us
  transfers between devices with their start and end apart: 8, of which 8 were waited for; matrix products, arithmetic and copies ran while one was open for 6% of the time, Pallas kernels for 0%

commit v1 on v0

v1 whole, which is shorter than its diff:
```python
import jax
import jax.numpy as jnp
from jax import lax
from jax.experimental import pallas as pl
from jax.experimental.pallas import tpu as pltpu
from jax.sharding import PartitionSpec as P

MESH = pl.DeviceIdType.MESH
BF = jnp.bfloat16
F32 = jnp.float32
N = 8
ROWS = 64
DM = 384
QW = 1152
FW = 1536
CH = 768
QA = 640
QB = 512
COPIES = 160


def dot_bt(a, b):
    return lax.dot_general(a, b, (((1,), (1,)), ((), ())), preferred_element_type=F32)


def dot_ta(a, b):
    return lax.dot_general(a, b, (((0,), (0,)), ((), ())), preferred_element_type=F32)


def dot(a, b):
    return jnp.dot(a, b, preferred_element_type=F32)


def wrap(i):
    return lax.rem(i + 2 * N, N)


def rows_of(slot, size, start=0, count=None):
    count = size if count is None else count
    return pl.ds(pl.multiple_of(slot * size + start, 16), count)


def kernel(
    n_in, g_in, q_in, p_in, wq_in, wu_in, wd_in,
    gi_out, gwq_out, gwu_out, gwd_out,
    normed, normed_t, grads, qkv, act, slope, w_down, w_up, w_qkv,
    part, part_r, part_l, gpre, summed, outgoing, in_x, in_z,
    d_part, d_sib, d_first, d_last,
    ua_part, ua_sib, ua_first, ua_last,
    ub_part, ub_sib, ub_first, ub_last,
    qa_part, qa_sib, qa_first, qa_last,
    qb_part, qb_sib, qb_first, qb_last,
    send_sems, recv_sems,
):
    gx, gy, gz = lax.axis_index("gx"), lax.axis_index("gy"), lax.axis_index("gz")
    core = lax.rem(gx, 2)
    chip = gx // 2
    z_lo, x = gz // 4, lax.rem(gz, 4)

    sib = (gx + 1 - 2 * core, gy, gz)
    chip_r, chip_l = (wrap(gx + 2), gy, gz), (wrap(gx - 2), gy, gz)
    up, down = (gx, wrap(gy + 1), gz), (gx, wrap(gy - 1), gz)
    zp = (gx, gy, wrap(gz + 4))

    def x_index(shift):
        return lax.rem(x + shift, 4)

    xs = [(gx, gy, z_lo * 4 + x_index(d)) for d in (1, 2, 3)]

    barrier = pltpu.get_barrier_semaphore()
    peers = [sib, chip_r, chip_l, up, down, zp] + xs
    for peer in peers:
        pl.semaphore_signal(barrier, inc=1, device_id=peer, device_id_type=MESH)

    started = []

    def send(src, dst, peer):
        i = len(started)
        copy = pltpu.make_async_remote_copy(
            src_ref=src, dst_ref=dst, send_sem=send_sems.at[i], recv_sem=recv_sems.at[i],
            device_id=peer, device_id_type=MESH,
        )
        copy.start()
        started.append(copy)
        return copy

    class ChipGather:
        def __init__(self, own, full, size):
            self.own, self.full, self.size = own, full, size

        def at(self, shift):
            return self.full.at[rows_of(wrap(gx + shift), self.size)]

        def half(self, shift, h):
            slot = wrap(gx + shift)
            if self.size % 32 == 0:
                return self.full.at[rows_of(slot, self.size, h * self.size // 2, self.size // 2)]
            width = self.full.shape[1] // 256 * 128
            cols = pl.ds(0, width) if h == 0 else pl.ds(width, self.full.shape[1] - width)
            return self.full.at[rows_of(slot, self.size), cols]

        def start(self):
            me = self.at(0)
            self.to_sib = [send(self.own, me, sib)]
            self.to_r = send(self.own, me, chip_r)
            self.to_l = send(self.own, me, chip_l)
            self.full[rows_of(gx, self.size)] = self.own[...]

        def forward(self):
            self.to_r.wait_recv()
            self.far_r = send(self.half(-2, 0), self.half(-2, 0), chip_r)
            self.to_l.wait_recv()
            self.far_l = send(self.half(2, 1), self.half(2, 1), chip_l)
            self.to_sib.append(send(self.at(-2), self.at(-2), sib))
            self.to_sib.append(send(self.at(2), self.at(2), sib))

        def finish(self):
            self.far_r.wait_recv()
            self.to_sib.append(send(self.half(4, 0), self.half(4, 0), sib))
            self.far_l.wait_recv()
            self.to_sib.append(send(self.half(4, 1), self.half(4, 1), sib))

        def complete(self):
            for copy in self.to_sib:
                copy.wait_recv()

    class RingGather:
        def __init__(self, full):
            self.full = full

        def at(self, shift, start=0, count=ROWS):
            return self.full.at[rows_of(wrap(gy + shift), ROWS, start, count)]

        def start(self):
            self.step = 0
            self.go_up = send(self.at(0), self.at(0), up)
            self.go_down = send(self.at(0), self.at(0), down)

        def forward(self):
            self.step += 1
            s = self.step
            start_up, start_down, count = (0, 0, ROWS) if s < 3 else (0, ROWS // 2, ROWS // 2)
            self.go_up.wait_recv()
            if s < 4:
                src = self.at(-s, start_up, count)
                self.go_up = send(src, src, up)
            self.go_down.wait_recv()
            if s < 4:
                src = self.at(s, start_down, count)
                self.go_down = send(src, src, down)

    class RingReduce:
        def __init__(self, c):
            self.c = c
            self.mine = part.at[c]

        def at(self, shift, start=0, count=ROWS):
            return rows_of(wrap(gy + shift), ROWS, start, count)

        def start(self):
            half = ROWS // 2
            self.step = 1
            self.go_up = send(self.mine.at[self.at(4, 0, half)], part_r.at[self.c, 0, pl.ds(0, half)], up)
            self.go_down = send(self.mine.at[self.at(4, half, half)], part_l.at[self.c, 0, pl.ds(half, half)], down)

        def add(self, rows, other):
            self.mine[rows] = (self.mine[rows].astype(F32) + other.astype(F32)).astype(BF)

        def forward(self):
            s = self.step
            half = ROWS // 2
            self.go_up.wait_recv()
            if s == 1:
                self.add(self.at(3, 0, half), part_r[self.c, 0, 0:half])
            else:
                self.add(self.at(4 - s), part_r[self.c, s - 1])
            self.go_up = send(self.mine.at[self.at(4 - s)], part_r.at[self.c, s], up)
            self.go_down.wait_recv()
            if s == 1:
                self.add(self.at(-3, half, half), part_l[self.c, 0, half:ROWS])
            else:
                self.add(self.at(s - 4), part_l[self.c, s - 1])
            self.go_down = send(self.mine.at[self.at(s - 4)], part_l.at[self.c, s], down)
            self.step += 1

        def finish(self):
            self.go_up.wait_recv()
            self.go_down.wait_recv()
            c = self.c

            def body(i, carry):
                r = pl.ds(pl.multiple_of(i * 16, 16), 16)
                rows = rows_of(gy, ROWS, i * 16, 16)
                total = self.mine[rows].astype(F32) + part_r[c, 3, r].astype(F32) + part_l[c, 3, r].astype(F32)
                gpre[c, rows] = (total * slope[r, CH * c : CH * c + CH]).astype(BF)
                return carry

            lax.fori_loop(0, ROWS // 16, body, 0)

    class PlaneGather:
        def __init__(self, own, full):
            self.own, self.full = own, full

        def at(self, shift):
            return self.full.at[rows_of(wrap(gz + shift), ROWS)]

        def start(self):
            self.to_z = send(self.own, self.at(0), zp)
            self.to_x = [send(self.own, self.at(0), peer) for peer in xs]
            self.full[rows_of(gz, ROWS)] = self.own[...]

        def forward(self):
            self.to_z.wait_recv()
            self.to_x += [send(self.at(4), self.at(4), peer) for peer in xs]

        def complete(self):
            for copy in self.to_x:
                copy.wait_recv()

    class ChipReduce:
        def __init__(self, halves):
            self.halves = halves

        def start(self):
            self.swap = [send(p.at[1 - core], s, sib) for p, s, _, _ in self.halves]

        def total(self, h, k):
            p, s, _, _ = self.halves[h]
            return p[core, k].astype(F32) + s[k].astype(F32)

        def put(self, h, k, value):
            self.halves[h][0][core, k] = value.astype(BF)

        def chips(self):
            for copy in self.swap:
                copy.wait_recv()
            far, right, left = (lax.rem(chip + i, 4) for i in (2, 1, 3))
            (pa, _, fa, la), (pb, _, fb, lb) = self.halves
            self.put(0, far, self.total(0, far))
            self.far_r = send(pa.at[core, far], fa, chip_r)
            self.put(1, far, self.total(1, far))
            self.far_l = send(pb.at[core, far], fb, chip_l)
            self.put(1, right, self.total(1, right))
            self.near = [send(pb.at[core, right], lb.at[0], chip_r)]
            self.put(0, left, self.total(0, left))
            self.near.append(send(pa.at[core, left], la.at[1], chip_l))

        def forward(self):
            right, left = (lax.rem(chip + i, 4) for i in (1, 3))
            (pa, _, fa, la), (pb, _, fb, lb) = self.halves
            self.far_r.wait_recv()
            self.put(0, right, self.total(0, right) + fa[...].astype(F32))
            self.near.append(send(pa.at[core, right], la.at[0], chip_r))
            self.far_l.wait_recv()
            self.put(1, left, self.total(1, left) + fb[...].astype(F32))
            self.near.append(send(pb.at[core, left], lb.at[1], chip_l))

        def finish(self, store):
            for copy in self.near:
                copy.wait_recv()
            for h in (0, 1):
                last = self.halves[h][3]
                store(h, (self.total(h, chip) + last[0].astype(F32) + last[1].astype(F32)).astype(BF))

    def gelu():
        def body(i, carry):
            r = pl.ds(pl.multiple_of(i * 16, 16), 16)
            for c in range(0, FW, DM):
                v = p_in[r, c : c + DM].astype(F32)
                cdf = 0.5 * (1.0 + lax.erf(v * 0.7071067811865476))
                pdf = jnp.exp(-0.5 * v * v) * 0.3989422804014327
                act[rows_of(gy, ROWS, i * 16, 16), c : c + DM] = (v * cdf).astype(BF)
                slope[r, c : c + DM] = cdf + v * pdf
            return carry

        lax.fori_loop(0, ROWS // 16, body, 0)

    def partial_act(c):
        def body(i, carry):
            r = pl.ds(pl.multiple_of(i * 256, 256), 256)
            part[c, r] = dot_bt(grads[r], w_down[c * CH : c * CH + CH]).astype(BF)
            return carry

        lax.fori_loop(0, 2, body, 0)

    def grad_down():
        def body(k, carry):
            cols = pl.ds(pl.multiple_of(k * DM, DM), DM)
            product = dot_ta(act[:, cols], grads[...]).astype(BF)
            for c in (0, 1):
                for h in (0, 1):
                    at = 192 * c + 96 * h
                    d_part[h, c, k] = product[at : at + 96]
            return carry

        lax.fori_loop(0, 4, body, 0)

    def split(product, target):
        for g in range(N):
            target[g % 2, g // 2] = product[48 * g : 48 * g + 48]

    def grad_qkv():
        split(dot(normed_t[...], qkv[:, 0:QA]).astype(BF), qa_part)
        split(dot(normed_t[...], qkv[:, QA:QW]).astype(BF), qb_part)

    def grad_up(c):
        target = (ua_part, ub_part)[c]
        for h in (0, 1):
            split(dot(normed_t[...], gpre[c, :, h * DM : h * DM + DM]).astype(BF), target.at[h])

    def input_qkv():
        def body(i, carry):
            r = pl.ds(pl.multiple_of(i * 256, 256), 256)
            summed[r] = dot_bt(qkv[r], w_qkv[...])
            return carry

        lax.fori_loop(0, 2, body, 0)

    def input_up():
        def body(i, carry):
            r = pl.ds(pl.multiple_of(i * 256, 256), 256)
            total = summed[r]
            for c in (0, 1):
                total = total + dot_bt(gpre[c, r], w_up[:, c * CH : c * CH + CH])
            outgoing[r] = total.astype(BF)
            return carry

        lax.fori_loop(0, 2, body, 0)

    plane = {}

    def plane_start():
        plane["x"] = [
            send(outgoing.at[rows_of(z * 4 + x_index(d), ROWS)], in_x.at[d - 1, z], xs[d - 1])
            for d in (1, 2, 3)
            for z in (0, 1)
        ]

    def plane_total(z):
        total = outgoing[rows_of(z * 4 + x, ROWS)].astype(F32)
        for d in range(3):
            total = total + in_x[d, z].astype(F32)
        return total

    def plane_forward():
        for copy in plane["x"]:
            copy.wait_recv()
        rows = rows_of((1 - z_lo) * 4 + x, ROWS)
        outgoing[rows] = plane_total(1 - z_lo).astype(BF)
        plane["z"] = send(outgoing.at[rows], in_z, zp)

    def plane_finish():
        plane["z"].wait_recv()
        gi_out[...] = (plane_total(z_lo) + in_z[...].astype(F32)).astype(BF)

    def store_down(h, value):
        gwd_out[96 * h : 96 * h + 96] = value

    def store_qkv(h, value):
        cols = slice(0, QA) if h == 0 else slice(QA, QW)
        gwq_out[:, cols] = value

    def store_up(c):
        def store(h, value):
            at = c * CH + h * DM
            gwu_out[:, at : at + DM] = value

        return store

    wd, wu, wq = ChipGather(wd_in, w_down, 192), ChipGather(wu_in, w_up, 48), ChipGather(wq_in, w_qkv, 48)
    ga, gq, gp = RingGather(act), RingGather(qkv), [RingGather(gpre.at[c]) for c in (0, 1)]
    rr = [RingReduce(c) for c in (0, 1)]
    pg, pn = PlaneGather(g_in, grads), PlaneGather(n_in, normed)
    rd = ChipReduce([(d_part.at[h], d_sib.at[h], d_first.at[h], d_last.at[h]) for h in (0, 1)])
    ru = [
        ChipReduce([(p.at[h], s.at[h], f.at[h], t.at[h]) for h in (0, 1)])
        for p, s, f, t in ((ua_part, ua_sib, ua_first, ua_last), (ub_part, ub_sib, ub_first, ub_last))
    ]
    rq = ChipReduce([(qa_part, qa_sib, qa_first, qa_last), (qb_part, qb_sib, qb_first, qb_last)])

    qkv[rows_of(gy, ROWS)] = q_in[...]
    gelu()
    pl.semaphore_wait(barrier, len(peers))

    pg.start()
    wd.start()
    ga.start()
    gq.start()
    pn.start()
    pg.forward()
    pn.forward()
    ga.forward()
    wd.forward()
    wu.start()
    gq.forward()
    pg.complete()
    ga.forward()
    wd.finish()
    wd.complete()
    partial_act(0)
    rr[0].start()
    partial_act(1)
    rr[1].start()
    gq.forward()
    wu.forward()
    wq.start()
    pn.complete()
    normed_t[...] = normed[...].T
    rr[0].forward()
    rr[1].forward()
    ga.forward()
    wu.finish()
    rr[0].forward()
    rr[1].forward()
    gq.forward()
    wq.forward()
    ga.forward()
    rr[0].forward()
    rr[1].forward()
    grad_down()
    rd.start()
    rr[0].finish()
    gp[0].start()
    rr[1].finish()
    gp[1].start()
    rd.chips()
    wq.finish()
    gq.forward()
    gp[0].forward()
    gp[1].forward()
    grad_qkv()
    rq.start()
    rd.forward()
    gp[0].forward()
    gp[1].forward()
    rq.chips()
    wq.complete()
    input_qkv()
    rd.finish(store_down)
    gp[0].forward()
    gp[1].forward()
    rq.forward()
    wu.complete()
    gp[0].forward()
    grad_up(0)
    ru[0].start()
    gp[1].forward()
    grad_up(1)
    ru[1].start()
    ru[0].chips()
    input_up()
    plane_start()
    ru[1].chips()
    rq.finish(store_qkv)
    ru[0].forward()
    ru[1].forward()
    plane_forward()
    ru[0].finish(store_up(0))
    plane_finish()
    ru[1].finish(store_up(1))
    for copy in started:
        copy.wait_send()


def reduce_scratch(rows, width, halves=None):
    lead = () if halves is None else (halves,)
    return [
        pltpu.VMEM(lead + (2, 4, rows, width), BF),
        pltpu.VMEM(lead + (4, rows, width), BF),
        pltpu.VMEM(lead + (rows, width), BF),
        pltpu.VMEM(lead + (2, rows, width), BF),
    ]


def shards(normed, grad_out, grad_qkv_out, pre_act, w_qkv, w_up, w_down):
    outs = (normed, w_qkv, w_up, w_down)
    return pl.pallas_call(
        kernel,
        out_shape=[jax.ShapeDtypeStruct(o.shape, BF) for o in outs],
        in_specs=[pl.BlockSpec(memory_space=pltpu.VMEM)] * 7,
        out_specs=[pl.BlockSpec(memory_space=pltpu.VMEM)] * 4,
        scratch_shapes=[
            pltpu.VMEM((N * ROWS, DM), BF),
            pltpu.VMEM((DM, N * ROWS), BF),
            pltpu.VMEM((N * ROWS, DM), BF),
            pltpu.VMEM((N * ROWS, QW), BF),
            pltpu.VMEM((N * ROWS, FW), BF),
            pltpu.VMEM((ROWS, FW), F32),
            pltpu.VMEM((FW, DM), BF),
            pltpu.VMEM((DM, FW), BF),
            pltpu.VMEM((DM, QW), BF),
            pltpu.VMEM((2, N * ROWS, CH), BF),
            pltpu.VMEM((2, 4, ROWS, CH), BF),
            pltpu.VMEM((2, 4, ROWS, CH), BF),
            pltpu.VMEM((2, N * ROWS, CH), BF),
            pltpu.VMEM((N * ROWS, DM), F32),
            pltpu.VMEM((N * ROWS, DM), BF),
            pltpu.VMEM((3, 2, ROWS, DM), BF),
            pltpu.VMEM((ROWS, DM), BF),
            *reduce_scratch(96, DM, 2),
            *reduce_scratch(48, DM, 2),
            *reduce_scratch(48, DM, 2),
            *reduce_scratch(48, QA),
            *reduce_scratch(48, QB),
            pltpu.SemaphoreType.DMA((COPIES,)),
            pltpu.SemaphoreType.DMA((COPIES,)),
        ],
        compiler_params=pltpu.CompilerParams(
            collective_id=0, has_side_effects=True, vmem_limit_bytes=48 << 20
        ),
    )(normed, grad_out, grad_qkv_out, pre_act, w_qkv, w_up, w_down)


def solution(mesh):
    rows, tall = P(("gx", "gz"), "gy"), P(("gx", "gy"), "gz")
    block, flat = P(("gy", "gx"), "gz"), P(("gz", "gx"), "gy")
    return jax.shard_map(
        shards,
        mesh=mesh,
        in_specs=(rows, rows, tall, tall, block, block, flat),
        out_specs=(rows, block, block, flat),
        check_vma=False,
    )
```

time: 402 us -> 104 us (0.26)
  waiting for transfers between devices: 288 us -> 0 us
  Pallas kernels: 0 us -> 93.9 us
  blocking collectives: 73.4 us -> 0 us
  matrix products: 13.9 us -> 0 us
  between operations: 14.2 us -> 0.66 us
    pallas_call x0 -> x1, Pallas kernels: none -> 93.9 us  [shards(): pl.pallas_call(kernel, out_shape=[jax.ShapeDtypeStruct(o.shape, BF) for o...]
    reduce_scatter x2 -> x0, waiting for transfers between devices: 87.7 us -> none  [the longest x1 48.4 us: shards(): lax.psum_scatter(weight_term(activated, grad_rows).astype(jnp.bfloat16),...]
    psum x1 -> x0, waiting for transfers between devices: 85.8 us -> none  [shards(): lax.psum(partial_act.astype(jnp.bfloat16), 'gy').astype(jnp.float32)]
    all_gather x3 -> x0, blocking collectives: 73.4 us -> none  [the longest x1 26.1 us: shards(): lax.all_gather(w_qkv, 'gx', axis=0, tiled=True)]
    all_gather x4 -> x0, waiting for transfers between devices: 73.1 us -> none  [the longest x1 38.6 us: shards(): lax.all_gather(grad_qkv_out, 'gy', axis=0, tiled=True)]
    unnamed x9 -> x0, waiting for transfers between devices: 41.9 us -> none
    dot_general x5 -> x0, matrix products: 13.9 us -> none  [the longest x3 8.38 us: dot_rows(): lax.dot_general(left, right, (((1,), (1,)), ((), ())), preferred_element_...]
    unnamed x11 -> x18, local copies, waits for them, and re-layouts: 3.35 us -> 8.73 us
  transfers between devices with their start and end apart: 8 -> 0, of which waited for: 8 -> 0; matrix products, arithmetic and copies ran while one was open for 6% -> 0% of each run, Pallas kernels for 0% -> 0%
where the time goes in v1:
time: 104 us; the launch traced here: 103 us
  Pallas kernels  93.9 us (90%)
  local copies, waits for them, and re-layouts  8.73 us (8%)
    pallas_call x1, Pallas kernels, shards(): pl.pallas_call(kernel, out_shape=[jax.ShapeDtypeStruct(o.shape, BF) for o...  93.9 us
    unnamed x18, local copies, waits for them, and re-layouts  8.73 us

profile of v1, /device:TPU:1, one launch (start us, length us, event | category | flops | bytes accessed | tf_op | source)
XLA Modules:
  0.0 103.3 jit_solution(7891989318380697430)
XLA Ops:
  0.6 0.0 copy-start
  0.6 0.9 copy-done
  1.6 0.0 copy-start.1
  1.6 0.9 copy-done.1
  2.5 0.0 copy-start.2
  2.5 0.9 copy-done.2
  3.4 0.0 copy-start.3
  3.4 0.9 copy-done.3
  4.3 0.0 copy-start.4
  4.3 0.9 copy-done.4
  5.2 0.0 copy-start.5
  5.2 0.8 copy-done.5
  6.0 0.0 copy-start.6
  6.0 0.8 copy-done.6
  6.8 93.9 %shard_map.102 = (bf16[64,384]{1,0:T(8,128)(2,1)S(1)}, bf16[48,1152]{1,0:T(8,128)(2,1)S(1)}, bf16[48,1536]{1,0:T(8,128)(2,1)S(1)}, bf16[192,384]{1,0:T(8,128)(2,1)S(1)}) custom-call(bf16[64,384]{1,0:T(8,128)(2,1)S(1)} %copy-done.5, bf16[64,384]{1,0:T(8,128)(2,1)S(1)} %copy-done.6, bf16[64,1152]{1,0:T(8,128)(2,1)S(1)} %copy-done.1, ...), custom_call_target="tpu_custom_call" | custom-call | tf_op jit(solution)/shard_map/pallas_call | solution.py:477
  100.7 0.6 copy.15
  101.3 0.6 copy.16
  102.0 0.7 copy.17
  102.6 0.7 copy.18
Async XLA Ops:
  0.6 0.9 copy-start
  1.6 0.9 copy-start.1
  2.5 0.9 copy-start.2
  3.4 0.9 copy-start.3
  4.3 0.9 copy-start.4
  5.2 0.8 copy-start.5
  6.0 0.8 copy-start.6

commit v2 on v1

v2 whole, which is shorter than its diff:
```python
import jax
import jax.numpy as jnp
from jax import lax
from jax.experimental import pallas as pl
from jax.experimental.pallas import tpu as pltpu
from jax.sharding import PartitionSpec as P

MESH = pl.DeviceIdType.MESH
BF = jnp.bfloat16
F32 = jnp.float32
N = 8
ROWS = 64
HALF = 32
DM = 384
QW = 1152
FW = 1536
QA = 640
QB = 512
WIDE = 256
COPIES = 200


def dot_bt(a, b):
    return lax.dot_general(a, b, (((1,), (1,)), ((), ())), preferred_element_type=F32)


def dot_ta(a, b):
    return lax.dot_general(a, b, (((0,), (0,)), ((), ())), preferred_element_type=F32)


def dot(a, b):
    return jnp.dot(a, b, preferred_element_type=F32)


def wrap(i):
    return lax.rem(i + 2 * N, N)


def rows_of(slot, size, start=0, count=None):
    count = size if count is None else count
    return pl.ds(pl.multiple_of(slot * size + start, 16), count)


def kernel(
    n_in, g_in, q_in, p_in, wq_in, wu_in, wd_in,
    gi_hbm, gwq_hbm, gwu_hbm, gwd_hbm,
    normed, normed_t, grads, qkv, act, slope, w_down, w_up, w_qkv,
    part, part_u, part_d, gpre, summed, outgoing, in_x, in_z,
    d_part, d_sib, d_first, d_last,
    uw_part, uw_sib, uw_first, uw_last,
    un_part, un_sib, un_first, un_last,
    qa_part, qa_sib, qa_first, qa_last,
    qb_part, qb_sib, qb_first, qb_last,
    pre, gi_out, gwq_out, gwu_out, gwd_out, send_sems, recv_sems, load_sems,
):
    gx, gy, gz = lax.axis_index("gx"), lax.axis_index("gy"), lax.axis_index("gz")
    core = lax.rem(gx, 2)
    chip = gx // 2
    z_lo, x = gz // 4, lax.rem(gz, 4)

    sib = (gx + 1 - 2 * core, gy, gz)
    chip_r, chip_l = (wrap(gx + 2), gy, gz), (wrap(gx - 2), gy, gz)
    up, down = (gx, wrap(gy + 1), gz), (gx, wrap(gy - 1), gz)
    zp = (gx, gy, wrap(gz + 4))

    def x_index(shift):
        return lax.rem(x + shift, 4)

    xs = [(gx, gy, z_lo * 4 + x_index(d)) for d in (1, 2, 3)]

    barrier = pltpu.get_barrier_semaphore()
    peers = [sib, chip_r, chip_l, up, down, zp] + xs
    for peer in peers:
        pl.semaphore_signal(barrier, inc=1, device_id=peer, device_id_type=MESH)

    loads = []

    def load(src, dst):
        copy = pltpu.make_async_copy(src, dst, load_sems.at[len(loads)])
        copy.start()
        loads.append(copy)
        return copy

    started = []

    class Send:
        def __init__(self, src, dst, peer):
            i = len(started)
            self.copy = pltpu.make_async_remote_copy(
                src_ref=src, dst_ref=dst, send_sem=send_sems.at[i], recv_sem=recv_sems.at[i],
                device_id=peer, device_id_type=MESH,
            )
            self.arrived = False
            self.copy.start()
            started.append(self)

        def wait(self):
            if not self.arrived:
                self.copy.wait_recv()
            self.arrived = True

    def wait_all(copies):
        for copy in copies:
            copy.wait()

    class ChipGather:
        def __init__(self, own, full, size, pieces):
            self.own, self.full, self.size, self.pieces = own, full, size, pieces
            self.to_sib = {}

        def half_at(self, h):
            if self.size % 32 == 0:
                return (pl.ds(h * self.size // 2, self.size // 2),)
            width = self.full.shape[1] // 256 * 128
            return (slice(None), pl.ds(0, width) if h == 0 else pl.ds(width, self.full.shape[1] - width))

        def at(self, shift):
            return self.full.at[rows_of(wrap(gx + shift), self.size)]

        def half(self, shift, h):
            return self.at(shift).at[self.half_at(h)]

        def start(self):
            if self.pieces:
                self.r, self.l = [None, None], [None, None]
                for h in (0, 1):
                    self.r[h] = Send(self.own.at[self.half_at(h)], self.half(0, h), chip_r)
                    self.l[1 - h] = Send(self.own.at[self.half_at(1 - h)], self.half(0, 1 - h), chip_l)
            else:
                self.r = [Send(self.own, self.at(0), chip_r)]
                self.l = [Send(self.own, self.at(0), chip_l)]
            self.to_sib["own"] = Send(self.own, self.at(0), sib)

        def fwd_r(self):
            self.r[0].wait()
            self.far_up = Send(self.half(-2, 0), self.half(-2, 0), chip_r)
            if not self.pieces:
                self.sh_r()

        def fwd_l(self):
            self.l[-1].wait()
            self.far_down = Send(self.half(2, 1), self.half(2, 1), chip_l)
            if not self.pieces:
                self.sh_l()

        def sh_r(self):
            wait_all(self.r)
            self.to_sib["r"] = Send(self.at(-2), self.at(-2), sib)

        def sh_l(self):
            wait_all(self.l)
            self.to_sib["l"] = Send(self.at(2), self.at(2), sib)

        def far_r(self):
            self.far_up.wait()
            self.to_sib["far_r"] = Send(self.half(4, 0), self.half(4, 0), sib)

        def far_l(self):
            self.far_down.wait()
            self.to_sib["far_l"] = Send(self.half(4, 1), self.half(4, 1), sib)

        def complete(self):
            for key in self.to_sib:
                self.to_sib[key].wait()

    class RingGather:
        def __init__(self, full, own=None):
            self.full, self.own = full, own
            self.chain = {}
            self.hops = {}

        def at(self, shift, h):
            return self.full.at[rows_of(wrap(gy + shift), ROWS, HALF * h, HALF)]

        def go(self, d, h):
            s = self.hops.get((d, h), 0)
            self.hops[d, h] = s + 1
            if s > 0:
                self.chain[d, h].wait()
            here = self.at(s if d else -s, h)
            src = self.own.at[pl.ds(HALF * h, HALF)] if s == 0 and self.own is not None else here
            self.chain[d, h] = Send(src, here, down if d else up)

        def complete(self):
            assert self.hops == {(0, 0): 4, (1, 1): 4, (0, 1): 3, (1, 0): 3}
            for key in self.chain:
                self.chain[key].wait()

    class BlockGather:
        def __init__(self, full):
            self.full = full

        def at(self, shift, start=0, count=ROWS):
            return self.full.at[rows_of(wrap(gy + shift), ROWS, start, count)]

        def start(self):
            self.step_u = self.step_d = 0
            self.to_u = Send(self.at(0), self.at(0), up)
            self.to_d = Send(self.at(0), self.at(0), down)

        def up(self):
            self.step_u += 1
            self.to_u.wait()
            src = self.at(-self.step_u, 0, ROWS if self.step_u < 3 else HALF)
            self.to_u = Send(src, src, up)

        def down(self):
            self.step_d += 1
            self.to_d.wait()
            src = self.at(self.step_d) if self.step_d < 3 else self.at(3, HALF, HALF)
            self.to_d = Send(src, src, down)

        def complete(self):
            assert self.step_u == self.step_d == 3
            self.to_u.wait()
            self.to_d.wait()

    class RingReduce:
        def __init__(self, rel):
            self.rel = rel
            self.block = lax.rem(chip + (0, 1, 3, 2)[rel], 4)
            self.mine = part.at[self.block]

        def at(self, shift, start=0, count=ROWS):
            return rows_of(wrap(gy + shift), ROWS, start, count)

        def start(self):
            pg.complete()
            if self.rel == 0:
                wd.to_sib["own"].wait()
            elif self.rel == 1:
                wait_all(wd.l + [wd.to_sib["l"]])
            elif self.rel == 2:
                wait_all(wd.r + [wd.to_sib["r"]])
            else:
                wait_all([wd.far_up, wd.far_down, wd.to_sib["far_r"], wd.to_sib["far_l"]])
            rows = rows_of(self.block, DM)

            def body(i, carry):
                r = pl.ds(pl.multiple_of(i * 256, 256), 256)
                self.mine[r] = dot_bt(grads[r], w_down[rows]).astype(BF)
                return carry

            lax.fori_loop(0, 2, body, 0)
            self.step_u = self.step_d = 1
            first = pl.ds(0, HALF), pl.ds(HALF, HALF)
            self.to_u = Send(self.mine.at[self.at(4, 0, HALF)], part_u.at[self.rel, 0, first[0]], up)
            self.to_d = Send(self.mine.at[self.at(4, HALF, HALF)], part_d.at[self.rel, 0, first[1]], down)

        def add(self, rows, other):
            self.mine[rows] = (self.mine[rows].astype(F32) + other.astype(F32)).astype(BF)

        def up(self):
            s = self.step_u
            self.step_u += 1
            self.to_u.wait()
            if s == 1:
                self.add(self.at(3, 0, HALF), part_u[self.rel, 0, 0:HALF])
            else:
                self.add(self.at(4 - s), part_u[self.rel, s - 1])
            self.to_u = Send(self.mine.at[self.at(4 - s)], part_u.at[self.rel, s], up)

        def down(self):
            s = self.step_d
            self.step_d += 1
            self.to_d.wait()
            if s == 1:
                self.add(self.at(-3, HALF, HALF), part_d[self.rel, 0, HALF:ROWS])
            else:
                self.add(self.at(s - 4), part_d[self.rel, s - 1])
            self.to_d = Send(self.mine.at[self.at(s - 4)], part_d.at[self.rel, s], down)

        def finish(self):
            assert self.step_u == self.step_d == 4
            self.to_u.wait()
            self.to_d.wait()
            rows = self.at(0)
            total = self.mine[rows].astype(F32) + part_u[self.rel, 3].astype(F32) + part_d[self.rel, 3].astype(F32)
            gpre[self.block, rows] = (total * slope[self.block]).astype(BF)

    class PlaneGather:
        def __init__(self, own, full):
            self.own, self.full = own, full

        def at(self, shift):
            return self.full.at[rows_of(wrap(gz + shift), ROWS)]

        def start(self):
            self.to_z = Send(self.own, self.at(0), zp)
            self.to_x = [Send(self.own, self.at(0), peer) for peer in xs]

        def forward(self):
            self.to_z.wait()
            self.to_x += [Send(self.at(4), self.at(4), peer) for peer in xs]

        def complete(self):
            wait_all(self.to_x)

    class ChipReduce:
        def __init__(self, halves, compute, store):
            self.halves, self.compute, self.store = halves, compute, store

        def start(self):
            self.compute()
            self.swap = [Send(p.at[1 - core], s, sib) for p, s, _, _ in self.halves]

        def total(self, h, k):
            p, s, _, _ = self.halves[h]
            return p[core, k].astype(F32) + s[k].astype(F32)

        def put(self, h, k, value):
            self.halves[h][0][core, k] = value.astype(BF)

        def chips(self):
            wait_all(self.swap)
            far, right, left = (lax.rem(chip + i, 4) for i in (2, 1, 3))
            (pa, _, fa, la), (pb, _, fb, lb) = self.halves
            self.put(0, far, self.total(0, far))
            self.far_up = Send(pa.at[core, far], fa, chip_r)
            self.put(1, far, self.total(1, far))
            self.far_down = Send(pb.at[core, far], fb, chip_l)
            self.put(1, right, self.total(1, right))
            self.near = [Send(pb.at[core, right], lb.at[0], chip_r)]
            self.put(0, left, self.total(0, left))
            self.near.append(Send(pa.at[core, left], la.at[1], chip_l))

        def fwd_r(self):
            right = lax.rem(chip + 1, 4)
            pa, _, fa, la = self.halves[0]
            self.far_up.wait()
            self.put(0, right, self.total(0, right) + fa[...].astype(F32))
            self.near.append(Send(pa.at[core, right], la.at[0], chip_r))

        def fwd_l(self):
            left = lax.rem(chip + 3, 4)
            pb, _, fb, lb = self.halves[1]
            self.far_down.wait()
            self.put(1, left, self.total(1, left) + fb[...].astype(F32))
            self.near.append(Send(pb.at[core, left], lb.at[1], chip_l))

        def finish(self):
            wait_all(self.near)
            for h in (0, 1):
                last = self.halves[h][3]
                self.store(h, (self.total(h, chip) + last[0].astype(F32) + last[1].astype(F32)).astype(BF))

    def gelu():
        def body(i, carry):
            r = pl.ds(pl.multiple_of(i * 16, 16), 16)
            for b in range(4):
                cols = slice(b * DM, b * DM + DM)
                v = pre[r, cols].astype(F32)
                cdf = 0.5 * (1.0 + lax.erf(v * 0.7071067811865476))
                pdf = jnp.exp(-0.5 * v * v) * 0.3989422804014327
                act[rows_of(gy, ROWS, i * 16, 16), cols] = (v * cdf).astype(BF)
                slope[b, r] = cdf + v * pdf
            return carry

        lax.fori_loop(0, ROWS // 16, body, 0)

    def tn():
        pn.complete()
        normed_t[...] = normed[...].T

    def grad_down():
        ga.complete()
        pg.complete()

        def body(k, carry):
            cols = pl.ds(pl.multiple_of(k * DM, DM), DM)
            product = dot_ta(act[:, cols], grads[...]).astype(BF)
            for c in (0, 1):
                for h in (0, 1):
                    at = 192 * c + 96 * h
                    d_part[h, c, k] = product[at : at + 96]
            return carry

        lax.fori_loop(0, 4, body, 0)

    def split(product, target):
        for g in range(N):
            target[g % 2, g // 2] = product[48 * g : 48 * g + 48]

    def grad_qkv():
        gq.complete()
        split(dot(normed_t[...], qkv[:, 0:QA]).astype(BF), qa_part)
        split(dot(normed_t[...], qkv[:, QA:QW]).astype(BF), qb_part)

    def grad_up(b):
        def run():
            gp[b].complete()
            product = dot(normed_t[...], gpre[b]).astype(BF)
            split(product[:, 0:WIDE], uw_part.at[b])
            split(product[:, WIDE:DM], un_part.at[b])

        return run

    def input_qkv():
        gq.complete()
        wq.complete()

        def body(i, carry):
            r = pl.ds(pl.multiple_of(i * 256, 256), 256)
            summed[r] = dot_bt(qkv[r], w_qkv[...])
            return carry

        lax.fori_loop(0, 2, body, 0)

    plane = {}

    def input_up():
        wu.complete()

        def body(i, carry):
            r = pl.ds(pl.multiple_of(i * 256, 256), 256)
            total = summed[r]
            for b in range(4):
                total = total + dot_bt(gpre[b, r], w_up[:, b * DM : b * DM + DM])
            outgoing[r] = total.astype(BF)
            return carry

        for b in range(4):
            gp[b].complete()
        lax.fori_loop(0, 2, body, 0)
        plane["x"] = [
            Send(outgoing.at[rows_of(z * 4 + x_index(d), ROWS)], in_x.at[d - 1, z], xs[d - 1])
            for d in (1, 2, 3)
            for z in (0, 1)
        ]

    def plane_total(z):
        total = outgoing[rows_of(z * 4 + x, ROWS)].astype(F32)
        for d in range(3):
            total = total + in_x[d, z].astype(F32)
        return total

    def plane_forward():
        wait_all(plane["x"])
        rows = rows_of((1 - z_lo) * 4 + x, ROWS)
        outgoing[rows] = plane_total(1 - z_lo).astype(BF)
        plane["z"] = Send(outgoing.at[rows], in_z, zp)

    def plane_finish():
        plane["z"].wait()
        gi_out[...] = (plane_total(z_lo) + in_z[...].astype(F32)).astype(BF)
        load(gi_out, gi_hbm)

    def store_down(h, value):
        gwd_out[96 * h : 96 * h + 96] = value
        if h == 1:
            load(gwd_out, gwd_hbm)

    def store_qkv(h, value):
        cols = slice(0, QA) if h == 0 else slice(QA, QW)
        gwq_out[:, cols] = value
        if h == 1:
            load(gwq_out, gwq_hbm)

    def store_up(b):
        def store(h, value):
            at = b * DM + (WIDE if narrow(b) == h else 0)
            gwu_out[:, at : at + value.shape[1]] = value
            if h == 1:
                cols = pl.ds(b * DM, DM)
                load(gwu_out.at[:, cols], gwu_hbm.at[:, cols])

        return store

    def narrow(b):
        return 1 - b % 2

    def up_halves(b):
        halves = [(uw_part.at[b], uw_sib.at[b], uw_first.at[b], uw_last.at[b]),
                  (un_part.at[b], un_sib.at[b], un_first.at[b], un_last.at[b])]
        return halves if b % 2 == 0 else halves[::-1]

    wd = ChipGather(wd_in, w_down, 192, True)
    wu, wq = ChipGather(wu_in, w_up, 48, False), ChipGather(wq_in, w_qkv, 48, False)
    ga, gq, gp = RingGather(act), RingGather(qkv, q_in), [BlockGather(gpre.at[b]) for b in range(4)]
    rr = [RingReduce(rel) for rel in range(4)]
    pg, pn = PlaneGather(g_in, grads), PlaneGather(n_in, normed)
    rd = ChipReduce([(d_part.at[h], d_sib.at[h], d_first.at[h], d_last.at[h]) for h in (0, 1)], grad_down, store_down)
    ru = [ChipReduce(up_halves(b), grad_up(b), store_up(b)) for b in range(4)]
    rq = ChipReduce([(qa_part, qa_sib, qa_first, qa_last), (qb_part, qb_sib, qb_first, qb_last)], grad_qkv, store_qkv)

    load_pre = load(p_in, pre)
    load(q_in, qkv.at[rows_of(gy, ROWS)])
    load(g_in, grads.at[rows_of(gz, ROWS)])
    load(wd_in, w_down.at[rows_of(gx, 192)])
    load(n_in, normed.at[rows_of(gz, ROWS)])
    load(wu_in, w_up.at[rows_of(gx, 48)])
    load(wq_in, w_qkv.at[rows_of(gx, 48)])
    load_pre.wait()
    gelu()
    for copy in loads[1:]:
        copy.wait()
    first_store = len(loads)
    pl.semaphore_wait(barrier, len(peers))

    ga.go(0,0)
    ga.go(1,1)
    ga.go(0,1)
    ga.go(1,0)
    wd.start()
    pg.start()
    pn.start()
    gq.go(0,0)
    gq.go(1,1)
    ga.go(0,0)
    ga.go(1,1)
    ga.go(0,1)
    ga.go(1,0)
    wd.fwd_r()
    wd.fwd_l()
    gq.go(0,1)
    gq.go(1,0)
    wd.sh_r()
    wd.sh_l()
    ga.go(0,0)
    ga.go(1,1)
    pg.forward()
    pn.forward()
    ga.go(0,1)
    ga.go(1,0)
    wu.start()
    wd.far_l()
    gq.go(0,0)
    gq.go(1,1)
    rr[0].start()
    ga.go(0,0)
    ga.go(1,1)
    wd.far_r()
    rr[1].start()
    rr[2].start()
    rr[3].start()
    rr[0].up()
    rr[0].down()
    tn()
    gq.go(0,1)
    gq.go(1,0)
    rd.start()
    rr[0].up()
    rr[0].down()
    rr[1].up()
    rr[1].down()
    rr[2].up()
    rr[2].down()
    rr[3].up()
    rr[3].down()
    wu.fwd_r()
    wu.fwd_l()
    rr[0].up()
    rd.chips()
    rr[0].down()
    rr[1].up()
    rr[1].down()
    rr[2].up()
    rr[2].down()
    rr[3].up()
    rr[3].down()
    gq.go(0,0)
    rr[0].finish()
    wu.far_r()
    wu.far_l()
    gq.go(1,1)
    rr[1].up()
    rr[1].down()
    rr[2].up()
    rr[2].down()
    rr[3].up()
    rr[3].down()
    rd.fwd_r()
    rd.fwd_l()
    gq.go(0,1)
    gq.go(1,0)
    rr[1].finish()
    gq.go(0,0)
    gq.go(1,1)
    rr[2].finish()
    rr[3].finish()
    gp[0].start()
    gp[1].start()
    gp[2].start()
    gp[3].start()
    wq.start()
    rd.finish()
    rq.start()
    gp[0].up()
    gp[0].down()
    gp[1].up()
    gp[1].down()
    gp[2].up()
    gp[2].down()
    gp[3].up()
    gp[3].down()
    rq.chips()
    gp[0].up()
    gp[0].down()
    wq.fwd_r()
    wq.fwd_l()
    gp[1].up()
    gp[1].down()
    gp[2].up()
    gp[2].down()
    gp[3].up()
    gp[3].down()
    gp[0].up()
    gp[0].down()
    rq.fwd_r()
    rq.fwd_l()
    gp[1].up()
    gp[1].down()
    gp[2].up()
    gp[2].down()
    gp[3].up()
    gp[3].down()
    ru[0].start()
    ru[1].start()
    ru[2].start()
    wq.far_r()
    wq.far_l()
    ru[3].start()
    ru[0].chips()
    ru[1].chips()
    ru[2].chips()
    rq.finish()
    input_qkv()
    input_up()
    ru[0].fwd_r()
    ru[0].fwd_l()
    ru[1].fwd_r()
    ru[1].fwd_l()
    ru[3].chips()
    ru[2].fwd_r()
    ru[2].fwd_l()
    ru[0].finish()
    ru[1].finish()
    ru[3].fwd_r()
    ru[3].fwd_l()
    plane_forward()
    ru[2].finish()
    ru[3].finish()
    plane_finish()
    for copy in loads[first_store:]:
        copy.wait()
    for sent in started:
        sent.copy.wait_send()


def reduce_scratch(rows, width, *lead):
    return [
        pltpu.VMEM(lead + (2, 4, rows, width), BF),
        pltpu.VMEM(lead + (4, rows, width), BF),
        pltpu.VMEM(lead + (rows, width), BF),
        pltpu.VMEM(lead + (2, rows, width), BF),
    ]


def shards(normed, grad_out, grad_qkv_out, pre_act, w_qkv, w_up, w_down):
    outs = (normed, w_qkv, w_up, w_down)
    return pl.pallas_call(
        kernel,
        out_shape=[jax.ShapeDtypeStruct(o.shape, BF) for o in outs],
        in_specs=[pl.BlockSpec(memory_space=pltpu.HBM)] * 7,
        out_specs=[pl.BlockSpec(memory_space=pltpu.HBM)] * 4,
        scratch_shapes=[
            pltpu.VMEM((N * ROWS, DM), BF),
            pltpu.VMEM((DM, N * ROWS), BF),
            pltpu.VMEM((N * ROWS, DM), BF),
            pltpu.VMEM((N * ROWS, QW), BF),
            pltpu.VMEM((N * ROWS, FW), BF),
            pltpu.VMEM((4, ROWS, DM), F32),
            pltpu.VMEM((FW, DM), BF),
            pltpu.VMEM((DM, FW), BF),
            pltpu.VMEM((DM, QW), BF),
            pltpu.VMEM((4, N * ROWS, DM), BF),
            pltpu.VMEM((4, 4, ROWS, DM), BF),
            pltpu.VMEM((4, 4, ROWS, DM), BF),
            pltpu.VMEM((4, N * ROWS, DM), BF),
            pltpu.VMEM((N * ROWS, DM), F32),
            pltpu.VMEM((N * ROWS, DM), BF),
            pltpu.VMEM((3, 2, ROWS, DM), BF),
            pltpu.VMEM((ROWS, DM), BF),
            *reduce_scratch(96, DM, 2),
            *reduce_scratch(48, WIDE, 4),
            *reduce_scratch(48, DM - WIDE, 4),
            *reduce_scratch(48, QA),
            *reduce_scratch(48, QB),
            pltpu.VMEM((ROWS, FW), BF),
            *[pltpu.VMEM(o.shape, BF) for o in outs],
            pltpu.SemaphoreType.DMA((COPIES,)),
            pltpu.SemaphoreType.DMA((COPIES,)),
            pltpu.SemaphoreType.DMA((16,)),
        ],
        compiler_params=pltpu.CompilerParams(
            collective_id=0, has_side_effects=True, vmem_limit_bytes=60 << 20
        ),
    )(normed, grad_out, grad_qkv_out, pre_act, w_qkv, w_up, w_down)


def solution(mesh):
    rows, tall = P(("gx", "gz"), "gy"), P(("gx", "gy"), "gz")
    block, flat = P(("gy", "gx"), "gz"), P(("gz", "gx"), "gy")
    return jax.shard_map(
        shards,
        mesh=mesh,
        in_specs=(rows, rows, tall, tall, block, block, flat),
        out_specs=(rows, block, block, flat),
        check_vma=False,
    )
```

time: 104 us -> 97.3 us (0.936)
  local copies, waits for them, and re-layouts: 8.73 us -> 4.64 us
  Pallas kernels: 93.9 us -> 91.8 us
    unnamed x18 -> x8, local copies, waits for them, and re-layouts: 8.73 us -> 4.64 us
    pallas_call x1, Pallas kernels: 93.9 us -> 91.8 us  [shards(): pl.pallas_call(kernel, out_shape=[jax.ShapeDtypeStruct(o.shape, BF) for o...]
where the time goes in v2:
time: 97.3 us; the launch traced here: 97.1 us
  Pallas kernels  91.8 us (94%)
  local copies, waits for them, and re-layouts  4.64 us (5%)
    pallas_call x1, Pallas kernels, shards(): pl.pallas_call(kernel, out_shape=[jax.ShapeDtypeStruct(o.shape, BF) for o...  91.8 us
    unnamed x8, local copies, waits for them, and re-layouts  4.64 us

profile of v2, /device:TPU:1, one launch (start us, length us, event | category | flops | bytes accessed | tf_op | source)
XLA Modules:
  0.0 97.1 jit_solution(2431865498577630648)
XLA Ops:
  0.6 91.8 %shard_map.102 = (bf16[64,384]{1,0:T(8,128)(2,1)}, bf16[48,1152]{1,0:T(8,128)(2,1)}, bf16[48,1536]{1,0:T(8,128)(2,1)}, bf16[192,384]{1,0:T(8,128)(2,1)}) custom-call(bf16[64,384]{1,0:T(8,128)(2,1)} %n_in.1, bf16[64,384]{1,0:T(8,128)(2,1)} %g_in.1, bf16[64,1152]{1,0:T(8,128)(2,1)} %q_in.1, bf16[64,1536]{1,0:T(8,128)(2,1)} %p_in.1, bf16[48,1152]{1,0:T(8,128)(2,1)} %wq_in.1, ...), custom_call_target="tpu_custom_call" | custom-call | tf_op jit(solution)/shard_map/pallas_call | solution.py:661
  92.4 0.0 copy-start.1
  92.4 1.5 %copy.15 = bf16[64,384]{1,0:T(8,128)(2,1)} copy(bf16[64,384]{1,0:T(8,128)(2,1)} %get-tuple-element.8) | data formatting | bytes 98304
  93.9 1.5 %copy.16 = bf16[48,1152]{1,0:T(8,128)(2,1)} copy(bf16[48,1152]{1,0:T(8,128)(2,1)} %get-tuple-element.9) | data formatting | bytes 221184
  95.4 0.0 copy-done.1
  95.4 0.0 copy-start
  95.4 0.7 copy.17
  96.1 0.3 copy-done
  96.4 0.7 copy.18
Async XLA Ops:
  92.4 3.0 %copy-start.1 = (bf16[48,1536]{1,0:T(8,128)(2,1)S(1)}, bf16[48,1536]{1,0:T(8,128)(2,1)}, u32[]{:S(2)}) copy-start(bf16[48,1536]{1,0:T(8,128)(2,1)} %get-tuple-element.10) | copy-start | bytes 442372
  95.4 1.0 copy-start

commit v3 on v2

v3 whole, which is shorter than its diff:
```python
import math

import jax
import jax.numpy as jnp
from jax import lax
from jax.experimental import pallas as pl
from jax.experimental.pallas import tpu as pltpu
from jax.sharding import PartitionSpec as P

MESH = pl.DeviceIdType.MESH
BF = jnp.bfloat16
F32 = jnp.float32
N = 8
ROWS = 64
HALF = 32
DM = 384
QW = 1152
FW = 1536
QA = 640
QB = 512
WIDE = 256
COPIES = 143
RING, CHIP, CORE, PLANE = range(4)
LINKS = 4


def dot_bt(a, b):
    return lax.dot_general(a, b, (((1,), (1,)), ((), ())), preferred_element_type=F32)


def dot_ta(a, b):
    return lax.dot_general(a, b, (((0,), (0,)), ((), ())), preferred_element_type=F32)


def dot(a, b):
    return jnp.dot(a, b, preferred_element_type=F32)


def wrap(i):
    return lax.rem(i + 2 * N, N)


def rows_of(slot, size, start=0, count=None):
    count = size if count is None else count
    return pl.ds(pl.multiple_of(slot * size + start, 16), count)


def kernel(
    n_in, g_in, q_in, p_in, wq_in, wu_in, wd_in,
    gi_out, gwq_out, gwu_out, gwd_out,
    normed, normed_t, grads, qkv, act, slope, w_down, w_up, w_qkv,
    part, part_u, part_d, gpre, summed, outgoing, in_x, in_z,
    d_part, d_sib, d_first, d_last,
    uw_part, uw_sib, uw_first, uw_last,
    un_part, un_sib, un_first, un_last,
    qa_part, qa_sib, qa_first, qa_last,
    qb_part, qb_sib, qb_first, qb_last,
    pre, size_ref, send_sems, recv_sems, load_sems,
):
    gx, gy, gz = lax.axis_index("gx"), lax.axis_index("gy"), lax.axis_index("gz")
    core = lax.rem(gx, 2)
    chip = gx // 2
    z_lo, x = gz // 4, lax.rem(gz, 4)

    sib = (gx + 1 - 2 * core, gy, gz)
    chip_r, chip_l = (wrap(gx + 2), gy, gz), (wrap(gx - 2), gy, gz)
    up, down = (gx, wrap(gy + 1), gz), (gx, wrap(gy - 1), gz)
    zp = (gx, gy, wrap(gz + 4))

    def x_index(shift):
        return lax.rem(x + shift, 4)

    xs = [(gx, gy, z_lo * 4 + x_index(d)) for d in (1, 2, 3)]

    barrier = pltpu.get_barrier_semaphore()
    peers = [sib, chip_r, chip_l, up, down, zp] + xs
    for peer in peers:
        pl.semaphore_signal(barrier, inc=1, device_id=peer, device_id_type=MESH)

    loads = []

    def load(src, dst):
        copy = pltpu.make_async_copy(src, dst, load_sems.at[len(loads)])
        copy.start()
        loads.append(copy)
        return copy

    sent = [0] * LINKS
    landings = []

    def wait_bytes(count, sem):
        piece = size_ref.at[pl.ds(0, count // 256)]
        pltpu.make_async_copy(piece, piece, sem).wait()

    class Landing:
        def __init__(self):
            self.sem = recv_sems.at[len(landings)]
            self.bytes = 0
            self.done = False
            landings.append(self)

        def wait(self):
            if not self.done:
                wait_bytes(self.bytes, self.sem)
            self.done = True

    def send(src, dst, peer, link, landing=None):
        landing = Landing() if landing is None else landing
        assert not landing.done
        pltpu.make_async_remote_copy(
            src_ref=src, dst_ref=dst, send_sem=send_sems.at[link], recv_sem=landing.sem,
            device_id=peer, device_id_type=MESH,
        ).start()
        size = 2 * math.prod(src.shape)
        landing.bytes += size
        sent[link] += size
        return landing

    def wait_all(copies):
        for copy in copies:
            copy.wait()

    class ChipGather:
        def __init__(self, own, full, size):
            self.own, self.full, self.size = own, full, size
            self.to_sib = Landing()
            self.count = 0

        def half_at(self, h):
            if self.size % 32 == 0:
                return (pl.ds(h * self.size // 2, self.size // 2),)
            width = self.full.shape[1] // 256 * 128
            return (slice(None), pl.ds(0, width) if h == 0 else pl.ds(width, self.full.shape[1] - width))

        def at(self, shift):
            return self.full.at[rows_of(wrap(gx + shift), self.size)]

        def half(self, shift, h):
            return self.at(shift).at[self.half_at(h)]

        def share(self, src, dst):
            self.count += 1
            send(src, dst, sib, CORE, self.to_sib)

        def start_a(self):
            self.r = [send(self.own.at[self.half_at(0)], self.half(0, 0), chip_r, CHIP)]
            self.l = [send(self.own.at[self.half_at(1)], self.half(0, 1), chip_l, CHIP)]
            self.share(self.own, self.at(0))

        def start_b(self):
            self.r.append(send(self.own.at[self.half_at(1)], self.half(0, 1), chip_r, CHIP))
            self.l.append(send(self.own.at[self.half_at(0)], self.half(0, 0), chip_l, CHIP))

        def fwd_r(self):
            self.r[0].wait()
            self.far_up = send(self.half(-2, 0), self.half(-2, 0), chip_r, CHIP)

        def fwd_l(self):
            self.l[0].wait()
            self.far_down = send(self.half(2, 1), self.half(2, 1), chip_l, CHIP)

        def sh_r(self):
            wait_all(self.r)
            self.share(self.at(-2), self.at(-2))

        def sh_l(self):
            wait_all(self.l)
            self.share(self.at(2), self.at(2))

        def far_r(self):
            self.far_up.wait()
            self.share(self.half(4, 0), self.half(4, 0))

        def far_l(self):
            self.far_down.wait()
            self.share(self.half(4, 1), self.half(4, 1))

        def complete(self):
            assert self.count == 5
            self.to_sib.wait()

    class RingGather:
        def __init__(self, full, own=None):
            self.full, self.own = full, own
            self.chain = {}
            self.hops = {}

        def at(self, shift, h):
            return self.full.at[rows_of(wrap(gy + shift), ROWS, HALF * h, HALF)]

        def go(self, d, h):
            s = self.hops.get((d, h), 0)
            self.hops[d, h] = s + 1
            if s > 0:
                self.chain[d, h].wait()
            here = self.at(s if d else -s, h)
            src = self.own.at[pl.ds(HALF * h, HALF)] if s == 0 and self.own is not None else here
            self.chain[d, h] = send(src, here, down if d else up, RING)

        def complete(self):
            assert self.hops == {(0, 0): 4, (1, 1): 4, (0, 1): 3, (1, 0): 3}
            for key in self.chain:
                self.chain[key].wait()

    class BlockGather:
        def __init__(self, full):
            self.full = full

        def at(self, shift, start=0, count=ROWS):
            return self.full.at[rows_of(wrap(gy + shift), ROWS, start, count)]

        def start(self):
            self.step_u = self.step_d = 0
            self.to_u = send(self.at(0), self.at(0), up, RING)
            self.to_d = send(self.at(0), self.at(0), down, RING)

        def up(self):
            self.step_u += 1
            self.to_u.wait()
            src = self.at(-self.step_u, 0, ROWS if self.step_u < 3 else HALF)
            self.to_u = send(src, src, up, RING)

        def down(self):
            self.step_d += 1
            self.to_d.wait()
            src = self.at(self.step_d) if self.step_d < 3 else self.at(3, HALF, HALF)
            self.to_d = send(src, src, down, RING)

        def complete(self):
            assert self.step_u == self.step_d == 3
            self.to_u.wait()
            self.to_d.wait()

    class RingReduce:
        def __init__(self, block):
            self.block = block
            self.mine = part.at[self.block]

        def at(self, shift, start=0, count=ROWS):
            return rows_of(wrap(gy + shift), ROWS, start, count)

        def start(self):
            pg.complete()
            wd.complete()
            rows = rows_of(self.block, DM)

            def body(i, carry):
                r = pl.ds(pl.multiple_of(i * 256, 256), 256)
                self.mine[r] = dot_bt(grads[r], w_down[rows]).astype(BF)
                return carry

            lax.fori_loop(0, 2, body, 0)
            self.step_u = self.step_d = 1
            first = pl.ds(0, HALF), pl.ds(HALF, HALF)
            self.to_u = send(self.mine.at[self.at(4, 0, HALF)], part_u.at[self.block, 0, first[0]], up, RING)
            self.to_d = send(self.mine.at[self.at(4, HALF, HALF)], part_d.at[self.block, 0, first[1]], down, RING)

        def add(self, rows, other):
            self.mine[rows] = (self.mine[rows].astype(F32) + other.astype(F32)).astype(BF)

        def up(self):
            s = self.step_u
            self.step_u += 1
            self.to_u.wait()
            if s == 1:
                self.add(self.at(3, 0, HALF), part_u[self.block, 0, 0:HALF])
            else:
                self.add(self.at(4 - s), part_u[self.block, s - 1])
            self.to_u = send(self.mine.at[self.at(4 - s)], part_u.at[self.block, s], up, RING)

        def down(self):
            s = self.step_d
            self.step_d += 1
            self.to_d.wait()
            if s == 1:
                self.add(self.at(-3, HALF, HALF), part_d[self.block, 0, HALF:ROWS])
            else:
                self.add(self.at(s - 4), part_d[self.block, s - 1])
            self.to_d = send(self.mine.at[self.at(s - 4)], part_d.at[self.block, s], down, RING)

        def finish(self):
            assert self.step_u == self.step_d == 4
            self.to_u.wait()
            self.to_d.wait()
            rows = self.at(0)
            total = self.mine[rows].astype(F32) + part_u[self.block, 3].astype(F32) + part_d[self.block, 3].astype(F32)
            gpre[self.block, rows] = (total * slope[self.block]).astype(BF)

    class PlaneGather:
        def __init__(self, own, full):
            self.own, self.full = own, full

        def at(self, shift):
            return self.full.at[rows_of(wrap(gz + shift), ROWS)]

        def start(self):
            self.to_z = send(self.own, self.at(0), zp, PLANE)
            self.to_x = Landing()
            self.spread(self.own, 0)

        def forward(self):
            self.to_z.wait()
            self.spread(self.at(4), 4)
            self.ready = True

        def spread(self, src, shift):
            for peer in xs:
                send(src, self.at(shift), peer, PLANE, self.to_x)

        def complete(self):
            assert self.ready
            self.to_x.wait()

    class ChipReduce:
        def __init__(self, halves, compute, store):
            self.halves, self.compute, self.store = halves, compute, store

        def start(self):
            self.compute()
            self.swap = Landing()
            for p, s, _, _ in self.halves:
                send(p.at[1 - core], s, sib, CORE, self.swap)

        def total(self, h, k):
            p, s, _, _ = self.halves[h]
            return p[core, k].astype(F32) + s[k].astype(F32)

        def put(self, h, k, value):
            self.halves[h][0][core, k] = value.astype(BF)

        def chips(self):
            self.swap.wait()
            far, right, left = (lax.rem(chip + i, 4) for i in (2, 1, 3))
            (pa, _, fa, la), (pb, _, fb, lb) = self.halves
            self.put(0, far, self.total(0, far))
            self.far_up = send(pa.at[core, far], fa, chip_r, CHIP)
            self.put(1, far, self.total(1, far))
            self.far_down = send(pb.at[core, far], fb, chip_l, CHIP)
            self.put(1, right, self.total(1, right))
            self.near = send(pb.at[core, right], lb.at[0], chip_r, CHIP)
            self.put(0, left, self.total(0, left))
            send(pa.at[core, left], la.at[1], chip_l, CHIP, self.near)

        def fwd_r(self):
            right = lax.rem(chip + 1, 4)
            pa, _, fa, la = self.halves[0]
            self.far_up.wait()
            self.put(0, right, self.total(0, right) + fa[...].astype(F32))
            send(pa.at[core, right], la.at[0], chip_r, CHIP, self.near)

        def fwd_l(self):
            left = lax.rem(chip + 3, 4)
            pb, _, fb, lb = self.halves[1]
            self.far_down.wait()
            self.put(1, left, self.total(1, left) + fb[...].astype(F32))
            send(pb.at[core, left], lb.at[1], chip_l, CHIP, self.near)

        def finish(self):
            self.near.wait()
            for h in (0, 1):
                last = self.halves[h][3]
                self.store(h, (self.total(h, chip) + last[0].astype(F32) + last[1].astype(F32)).astype(BF))

    def gelu():
        def body(i, carry):
            r = pl.ds(pl.multiple_of(i * 16, 16), 16)
            for b in range(4):
                cols = slice(b * DM, b * DM + DM)
                v = pre[r, cols].astype(F32)
                cdf = 0.5 * (1.0 + lax.erf(v * 0.7071067811865476))
                pdf = jnp.exp(-0.5 * v * v) * 0.3989422804014327
                act[rows_of(gy, ROWS, i * 16, 16), cols] = (v * cdf).astype(BF)
                slope[b, r] = cdf + v * pdf
            return carry

        lax.fori_loop(0, ROWS // 16, body, 0)

    def tn():
        pn.complete()
        normed_t[...] = normed[...].T

    def grad_down():
        ga.complete()
        pg.complete()

        def body(k, carry):
            cols = pl.ds(pl.multiple_of(k * DM, DM), DM)
            product = dot_ta(act[:, cols], grads[...]).astype(BF)
            for c in (0, 1):
                for h in (0, 1):
                    at = 192 * c + 96 * h
                    d_part[h, c, k] = product[at : at + 96]
            return carry

        lax.fori_loop(0, 4, body, 0)

    def split(product, target):
        for g in range(N):
            target[g % 2, g // 2] = product[48 * g : 48 * g + 48]

    def grad_qkv():
        gq.complete()
        split(dot(normed_t[...], qkv[:, 0:QA]).astype(BF), qa_part)
        split(dot(normed_t[...], qkv[:, QA:QW]).astype(BF), qb_part)

    def grad_up(b):
        def run():
            gp[b].complete()
            product = dot(normed_t[...], gpre[b]).astype(BF)
            split(product[:, 0:WIDE], uw_part.at[b])
            split(product[:, WIDE:DM], un_part.at[b])

        return run

    def input_qkv():
        gq.complete()
        wq.complete()

        def body(i, carry):
            r = pl.ds(pl.multiple_of(i * 256, 256), 256)
            summed[r] = dot_bt(qkv[r], w_qkv[...])
            return carry

        lax.fori_loop(0, 2, body, 0)

    plane = {}

    def input_up(b):
        gp[b].complete()
        wu.complete()

        def body(i, carry):
            r = pl.ds(pl.multiple_of(i * 256, 256), 256)
            total = summed[r] + dot_bt(gpre[b, r], w_up[:, b * DM : b * DM + DM])
            if b < 3:
                summed[r] = total
            else:
                outgoing[r] = total.astype(BF)
            return carry

        lax.fori_loop(0, 2, body, 0)

    def plane_start():
        plane["x"] = Landing()
        for d in (1, 2, 3):
            for z in (0, 1):
                rows = rows_of(z * 4 + x_index(d), ROWS)
                send(outgoing.at[rows], in_x.at[d - 1, z], xs[d - 1], PLANE, plane["x"])

    def plane_total(z):
        total = outgoing[rows_of(z * 4 + x, ROWS)].astype(F32)
        for d in range(3):
            total = total + in_x[d, z].astype(F32)
        return total

    def plane_forward():
        plane["x"].wait()
        rows = rows_of((1 - z_lo) * 4 + x, ROWS)
        outgoing[rows] = plane_total(1 - z_lo).astype(BF)
        plane["z"] = send(outgoing.at[rows], in_z, zp, PLANE)

    def plane_finish():
        plane["z"].wait()
        gi_out[...] = (plane_total(z_lo) + in_z[...].astype(F32)).astype(BF)

    def store_down(h, value):
        gwd_out[96 * h : 96 * h + 96] = value

    def store_qkv(h, value):
        cols = slice(0, QA) if h == 0 else slice(QA, QW)
        gwq_out[:, cols] = value

    def store_up(b):
        def store(h, value):
            at = b * DM + (WIDE if narrow(b) == h else 0)
            gwu_out[:, at : at + value.shape[1]] = value

        return store

    def narrow(b):
        return 1 - b % 2

    def up_halves(b):
        halves = [(uw_part.at[b], uw_sib.at[b], uw_first.at[b], uw_last.at[b]),
                  (un_part.at[b], un_sib.at[b], un_first.at[b], un_last.at[b])]
        return halves if b % 2 == 0 else halves[::-1]

    wd = ChipGather(wd_in, w_down, 192)
    wu, wq = ChipGather(wu_in, w_up, 48), ChipGather(wq_in, w_qkv, 48)
    ga, gq, gp = RingGather(act), RingGather(qkv, q_in), [BlockGather(gpre.at[b]) for b in range(4)]
    rr = [RingReduce(b) for b in range(4)]
    pg, pn = PlaneGather(g_in, grads), PlaneGather(n_in, normed)
    rd = ChipReduce([(d_part.at[h], d_sib.at[h], d_first.at[h], d_last.at[h]) for h in (0, 1)], grad_down, store_down)
    ru = [ChipReduce(up_halves(b), grad_up(b), store_up(b)) for b in range(4)]
    rq = ChipReduce([(qa_part, qa_sib, qa_first, qa_last), (qb_part, qb_sib, qb_first, qb_last)], grad_qkv, store_qkv)

    load_pre = load(p_in, pre)
    load(q_in, qkv.at[rows_of(gy, ROWS)])
    load(g_in, grads.at[rows_of(gz, ROWS)])
    load(wd_in, w_down.at[rows_of(gx, 192)])
    load(n_in, normed.at[rows_of(gz, ROWS)])
    load(wu_in, w_up.at[rows_of(gx, 48)])
    load(wq_in, w_qkv.at[rows_of(gx, 48)])
    load_pre.wait()
    gelu()
    for copy in loads[1:]:
        copy.wait()
    pl.semaphore_wait(barrier, len(peers))

    gq.go(0,0)
    gq.go(1,0)
    pn.start()
    gq.go(1,1)
    gq.go(0,1)
    pg.start()
    wd.start_a()
    ga.go(0,0)
    ga.go(1,0)
    wd.start_b()
    gq.go(0,0)
    gq.go(1,0)
    pn.forward()
    pg.forward()
    gq.go(1,1)
    gq.go(0,1)
    ga.go(0,1)
    ga.go(1,1)
    wd.fwd_l()
    wd.fwd_r()
    tn()
    gq.go(0,0)
    gq.go(1,0)
    gq.go(0,1)
    gq.go(1,1)
    wd.sh_l()
    wd.sh_r()
    ga.go(0,0)
    ga.go(1,0)
    wu.start_a()
    gq.go(0,0)
    ga.go(1,1)
    wd.far_l()
    wd.far_r()
    ga.go(0,1)
    wu.start_b()
    gq.go(1,1)
    rr[0].start()
    rr[1].start()
    rr[2].start()
    wq.start_a()
    ga.go(0,0)
    ga.go(1,0)
    wu.fwd_r()
    wu.fwd_l()
    rr[3].start()
    rq.start()
    rr[0].up()
    rr[0].down()
    rr[1].up()
    rr[1].down()
    wu.sh_r()
    rr[2].up()
    rr[2].down()
    wu.sh_l()
    rq.chips()
    wq.fwd_r()
    wq.fwd_l()
    ga.go(0,1)
    ga.go(1,1)
    rr[3].up()
    rr[3].down()
    rr[0].up()
    rr[0].down()
    rr[1].up()
    rr[1].down()
    wu.far_r()
    wu.far_l()
    rr[2].up()
    rr[2].down()
    rq.fwd_r()
    rq.fwd_l()
    ga.go(0,0)
    ga.go(1,1)
    rr[3].up()
    rr[3].down()
    rr[0].up()
    rr[0].down()
    rr[1].up()
    rr[1].down()
    rr[2].up()
    rr[2].down()
    wq.start_b()
    wq.far_r()
    wq.far_l()
    rd.start()
    rq.finish()
    rr[0].finish()
    gp[0].start()
    rr[3].up()
    rr[3].down()
    rr[1].finish()
    gp[1].start()
    rd.chips()
    rr[2].finish()
    gp[2].start()
    wq.sh_r()
    wq.sh_l()
    gp[0].up()
    gp[0].down()
    rr[3].finish()
    gp[3].start()
    input_qkv()
    gp[1].up()
    gp[1].down()
    gp[2].up()
    gp[2].down()
    gp[0].up()
    gp[0].down()
    gp[3].up()
    gp[3].down()
    rd.fwd_r()
    rd.fwd_l()
    gp[1].up()
    gp[1].down()
    gp[2].up()
    gp[2].down()
    gp[0].up()
    gp[0].down()
    gp[3].up()
    gp[3].down()
    gp[1].up()
    gp[1].down()
    gp[2].up()
    gp[2].down()
    ru[0].start()
    rd.finish()
    input_up(0)
    gp[3].up()
    gp[3].down()
    ru[1].start()
    ru[0].chips()
    ru[2].start()
    input_up(1)
    ru[1].chips()
    ru[3].start()
    ru[2].chips()
    input_up(2)
    input_up(3)
    plane_start()
    ru[3].chips()
    ru[0].fwd_r()
    ru[0].fwd_l()
    ru[1].fwd_r()
    ru[1].fwd_l()
    ru[2].fwd_r()
    ru[2].fwd_l()
    ru[3].fwd_r()
    ru[3].fwd_l()
    plane_forward()
    ru[0].finish()
    ru[1].finish()
    ru[2].finish()
    ru[3].finish()
    plane_finish()
    assert len(landings) <= COPIES
    for link in range(LINKS):
        wait_bytes(sent[link], send_sems.at[link])


def reduce_scratch(rows, width, *lead):
    return [
        pltpu.VMEM(lead + (2, 4, rows, width), BF),
        pltpu.VMEM(lead + (4, rows, width), BF),
        pltpu.VMEM(lead + (rows, width), BF),
        pltpu.VMEM(lead + (2, rows, width), BF),
    ]


def shards(normed, grad_out, grad_qkv_out, pre_act, w_qkv, w_up, w_down):
    ins, outs = (normed, grad_out, grad_qkv_out, pre_act, w_qkv, w_up, w_down), (normed, w_qkv, w_up, w_down)
    return pl.pallas_call(
        kernel,
        out_shape=[pltpu.VMEM(o.shape, BF) for o in outs],
        in_specs=[pl.BlockSpec(memory_space=pltpu.HBM)] * 7,
        out_specs=[pl.BlockSpec(memory_space=pltpu.VMEM)] * 4,
        scratch_shapes=[
            pltpu.VMEM((N * ROWS, DM), BF),
            pltpu.VMEM((DM, N * ROWS), BF),
            pltpu.VMEM((N * ROWS, DM), BF),
            pltpu.VMEM((N * ROWS, QW), BF),
            pltpu.VMEM((N * ROWS, FW), BF),
            pltpu.VMEM((4, ROWS, DM), F32),
            pltpu.VMEM((FW, DM), BF),
            pltpu.VMEM((DM, FW), BF),
            pltpu.VMEM((DM, QW), BF),
            pltpu.VMEM((4, N * ROWS, DM), BF),
            pltpu.VMEM((4, 4, ROWS, DM), BF),
            pltpu.VMEM((4, 4, ROWS, DM), BF),
            pltpu.VMEM((4, N * ROWS, DM), BF),
            pltpu.VMEM((N * ROWS, DM), F32),
            pltpu.VMEM((N * ROWS, DM), BF),
            pltpu.VMEM((3, 2, ROWS, DM), BF),
            pltpu.VMEM((ROWS, DM), BF),
            *reduce_scratch(96, DM, 2),
            *reduce_scratch(48, WIDE, 4),
            *reduce_scratch(48, DM - WIDE, 4),
            *reduce_scratch(48, QA),
            *reduce_scratch(48, QB),
            pltpu.VMEM((ROWS, FW), BF),
            pltpu.VMEM((24 << 10, 128), BF),
            pltpu.SemaphoreType.DMA((LINKS,)),
            pltpu.SemaphoreType.DMA((COPIES,)),
            pltpu.SemaphoreType.DMA((7,)),
        ],
        compiler_params=pltpu.CompilerParams(
            collective_id=0, has_side_effects=True, vmem_limit_bytes=48 << 20
        ),
    )(*[pltpu.with_memory_space_constraint(a, pltpu.HBM) for a in ins])


def solution(mesh):
    rows, tall = P(("gx", "gz"), "gy"), P(("gx", "gy"), "gz")
    block, flat = P(("gy", "gx"), "gz"), P(("gz", "gx"), "gy")
    return jax.shard_map(
        shards,
        mesh=mesh,
        in_specs=(rows, rows, tall, tall, block, block, flat),
        out_specs=(rows, block, block, flat),
        check_vma=False,
    )
```

time: 97.3 us -> 89.3 us (0.918)
  Pallas kernels: 91.8 us -> 85.5 us
  local copies, waits for them, and re-layouts: 4.64 us -> 2.59 us
    pallas_call x1, Pallas kernels: 91.8 us -> 85.5 us  [shards(): pl.pallas_call(kernel, out_shape=[pltpu.VMEM(o.shape, BF) for o in outs],...]
    unnamed x8 -> x4, local copies, waits for them, and re-layouts: 4.64 us -> 2.59 us
where the time goes in v3:
time: 89.3 us; the launch traced here: 88.8 us
  Pallas kernels  85.5 us (96%)
  local copies, waits for them, and re-layouts  2.59 us (3%)
    pallas_call x1, Pallas kernels, shards(): pl.pallas_call(kernel, out_shape=[pltpu.VMEM(o.shape, BF) for o in outs],...  85.5 us
    unnamed x4, local copies, waits for them, and re-layouts  2.59 us

profile of v3, /device:TPU:1, one launch (start us, length us, event | category | flops | bytes accessed | tf_op | source)
XLA Modules:
  0.0 88.8 jit_solution(3867822912624542536)
XLA Ops:
  0.6 85.5 %shard_map.102 = (bf16[64,384]{1,0:T(8,128)(2,1)S(1)}, bf16[48,1152]{1,0:T(8,128)(2,1)S(1)}, bf16[48,1536]{1,0:T(8,128)(2,1)S(1)}, bf16[192,384]{1,0:T(8,128)(2,1)S(1)}) custom-call(bf16[64,384]{1,0:T(8,128)(2,1)} %n_in.1, bf16[64,384]{1,0:T(8,128)(2,1)} %g_in.1, bf16[64,1152]{1,0:T(8,128)(2,1)} %q_in.1, bf16[64,1536]{1,0:T(8,128)(2,1)} %p_in.1, ...), custom_call_target="tpu_custom_call" | custom-call | tf_op jit(solution)/shard_map/pallas_call | solution.py:681
  86.2 0.6 copy.15
  86.8 0.6 copy.16
  87.5 0.7 copy.17
  88.1 0.7 copy.18

commit v4 on v3

--- a/solution.py
+++ b/solution.py
@@ -19,7 +19,7 @@
 QA = 640
 QB = 512
 WIDE = 256
-COPIES = 143
+COPIES = 84
 RING, CHIP, CORE, PLANE = range(4)
 LINKS = 4
 
@@ -143,36 +143,27 @@
             send(src, dst, sib, CORE, self.to_sib)
 
         def start_a(self):
-            self.r = [send(self.own.at[self.half_at(0)], self.half(0, 0), chip_r, CHIP)]
-            self.l = [send(self.own.at[self.half_at(1)], self.half(0, 1), chip_l, CHIP)]
+            self.a = send(self.own.at[self.half_at(0)], self.half(0, 0), chip_r, CHIP)
+            send(self.own.at[self.half_at(1)], self.half(0, 1), chip_l, CHIP, self.a)
             self.share(self.own, self.at(0))
 
         def start_b(self):
-            self.r.append(send(self.own.at[self.half_at(1)], self.half(0, 1), chip_r, CHIP))
-            self.l.append(send(self.own.at[self.half_at(0)], self.half(0, 0), chip_l, CHIP))
-
-        def fwd_r(self):
-            self.r[0].wait()
-            self.far_up = send(self.half(-2, 0), self.half(-2, 0), chip_r, CHIP)
-
-        def fwd_l(self):
-            self.l[0].wait()
-            self.far_down = send(self.half(2, 1), self.half(2, 1), chip_l, CHIP)
-
-        def sh_r(self):
-            wait_all(self.r)
+            self.b = send(self.own.at[self.half_at(1)], self.half(0, 1), chip_r, CHIP)
+            send(self.own.at[self.half_at(0)], self.half(0, 0), chip_l, CHIP, self.b)
+
+        def fwd(self):
+            self.a.wait()
+            self.c = send(self.half(-2, 0), self.half(-2, 0), chip_r, CHIP)
+            send(self.half(2, 1), self.half(2, 1), chip_l, CHIP, self.c)
+
+        def sh(self):
+            self.b.wait()
             self.share(self.at(-2), self.at(-2))
-
-        def sh_l(self):
-            wait_all(self.l)
             self.share(self.at(2), self.at(2))
 
-        def far_r(self):
-            self.far_up.wait()
+        def far(self):
+            self.c.wait()
             self.share(self.half(4, 0), self.half(4, 0))
-
-        def far_l(self):
-            self.far_down.wait()
             self.share(self.half(4, 1), self.half(4, 1))
 
         def complete(self):
@@ -188,19 +179,22 @@
         def at(self, shift, h):
             return self.full.at[rows_of(wrap(gy + shift), ROWS, HALF * h, HALF)]
 
-        def go(self, d, h):
-            s = self.hops.get((d, h), 0)
-            self.hops[d, h] = s + 1
+        def go(self, h):
+            s = self.hops.get(h, 0)
+            self.hops[h] = s + 1
             if s > 0:
-                self.chain[d, h].wait()
-            here = self.at(s if d else -s, h)
-            src = self.own.at[pl.ds(HALF * h, HALF)] if s == 0 and self.own is not None else here
-            self.chain[d, h] = send(src, here, down if d else up, RING)
+                self.chain[h].wait()
+            self.chain[h] = Landing()
+            for d, peer in ((0, up), (1, down)):
+                if s < 3 or d == h:
+                    here = self.at(s if d else -s, h)
+                    src = self.own.at[pl.ds(HALF * h, HALF)] if s == 0 and self.own is not None else here
+                    send(src, here, peer, RING, self.chain[h])
 
         def complete(self):
-            assert self.hops == {(0, 0): 4, (1, 1): 4, (0, 1): 3, (1, 0): 3}
-            for key in self.chain:
-                self.chain[key].wait()
+            assert self.hops == {0: 4, 1: 4}
+            for h in (0, 1):
+                self.chain[h].wait()
 
     class BlockGather:
         def __init__(self, full):
@@ -210,26 +204,23 @@
             return self.full.at[rows_of(wrap(gy + shift), ROWS, start, count)]
 
         def start(self):
-            self.step_u = self.step_d = 0
-            self.to_u = send(self.at(0), self.at(0), up, RING)
-            self.to_d = send(self.at(0), self.at(0), down, RING)
-
-        def up(self):
-            self.step_u += 1
-            self.to_u.wait()
-            src = self.at(-self.step_u, 0, ROWS if self.step_u < 3 else HALF)
-            self.to_u = send(src, src, up, RING)
-
-        def down(self):
-            self.step_d += 1
-            self.to_d.wait()
-            src = self.at(self.step_d) if self.step_d < 3 else self.at(3, HALF, HALF)
-            self.to_d = send(src, src, down, RING)
+            self.step = 0
+            self.go()
+
+        def go(self):
+            s = self.step
+            self.step += 1
+            if s > 0:
+                self.landing.wait()
+            self.landing = Landing()
+            src = self.at(-s, 0, ROWS if s < 3 else HALF)
+            send(src, src, up, RING, self.landing)
+            src = self.at(s) if s < 3 else self.at(3, HALF, HALF)
+            send(src, src, down, RING, self.landing)
 
         def complete(self):
-            assert self.step_u == self.step_d == 3
-            self.to_u.wait()
-            self.to_d.wait()
+            assert self.step == 4
+            self.landing.wait()
 
     class RingReduce:
         def __init__(self, block):
@@ -250,38 +241,30 @@
                 return carry
 
             lax.fori_loop(0, 2, body, 0)
-            self.step_u = self.step_d = 1
-            first = pl.ds(0, HALF), pl.ds(HALF, HALF)
-            self.to_u = send(self.mine.at[self.at(4, 0, HALF)], part_u.at[self.block, 0, first[0]], up, RING)
-            self.to_d = send(self.mine.at[self.at(4, HALF, HALF)], part_d.at[self.block, 0, first[1]], down, RING)
+            self.step = 1
+            half = self.at(4, 0, HALF), self.at(4, HALF, HALF)
+            self.landing = send(self.mine.at[half[0]], part_u.at[self.block, 0, pl.ds(0, HALF)], up, RING)
+            send(self.mine.at[half[1]], part_d.at[self.block, 0, pl.ds(HALF, HALF)], down, RING, self.landing)
 
         def add(self, rows, other):
             self.mine[rows] = (self.mine[rows].astype(F32) + other.astype(F32)).astype(BF)
 
-        def up(self):
-            s = self.step_u
-            self.step_u += 1
-            self.to_u.wait()
+        def go(self):
+            s = self.step
+            self.step += 1
+            self.landing.wait()
             if s == 1:
                 self.add(self.at(3, 0, HALF), part_u[self.block, 0, 0:HALF])
+                self.add(self.at(-3, HALF, HALF), part_d[self.block, 0, HALF:ROWS])
             else:
                 self.add(self.at(4 - s), part_u[self.block, s - 1])
-            self.to_u = send(self.mine.at[self.at(4 - s)], part_u.at[self.block, s], up, RING)
-
-        def down(self):
-            s = self.step_d
-            self.step_d += 1
-            self.to_d.wait()
-            if s == 1:
-                self.add(self.at(-3, HALF, HALF), part_d[self.block, 0, HALF:ROWS])
-            else:
                 self.add(self.at(s - 4), part_d[self.block, s - 1])
-            self.to_d = send(self.mine.at[self.at(s - 4)], part_d.at[self.block, s], down, RING)
+            self.landing = send(self.mine.at[self.at(4 - s)], part_u.at[self.block, s], up, RING)
+            send(self.mine.at[self.at(s - 4)], part_d.at[self.block, s], down, RING, self.landing)
 
         def finish(self):
-            assert self.step_u == self.step_d == 4
-            self.to_u.wait()
-            self.to_d.wait()
+            assert self.step == 4
+            self.landing.wait()
             rows = self.at(0)
             total = self.mine[rows].astype(F32) + part_u[self.block, 3].astype(F32) + part_d[self.block, 3].astype(F32)
             gpre[self.block, rows] = (total * slope[self.block]).astype(BF)
@@ -333,25 +316,20 @@
             far, right, left = (lax.rem(chip + i, 4) for i in (2, 1, 3))
             (pa, _, fa, la), (pb, _, fb, lb) = self.halves
             self.put(0, far, self.total(0, far))
-            self.far_up = send(pa.at[core, far], fa, chip_r, CHIP)
+            self.far = send(pa.at[core, far], fa, chip_r, CHIP)
             self.put(1, far, self.total(1, far))
-            self.far_down = send(pb.at[core, far], fb, chip_l, CHIP)
+            send(pb.at[core, far], fb, chip_l, CHIP, self.far)
             self.put(1, right, self.total(1, right))
             self.near = send(pb.at[core, right], lb.at[0], chip_r, CHIP)
             self.put(0, left, self.total(0, left))
             send(pa.at[core, left], la.at[1], chip_l, CHIP, self.near)
 
-        def fwd_r(self):
-            right = lax.rem(chip + 1, 4)
-            pa, _, fa, la = self.halves[0]
-            self.far_up.wait()
+        def fwd(self):
+            right, left = (lax.rem(chip + i, 4) for i in (1, 3))
+            (pa, _, fa, la), (pb, _, fb, lb) = self.halves
+            self.far.wait()
             self.put(0, right, self.total(0, right) + fa[...].astype(F32))
             send(pa.at[core, right], la.at[0], chip_r, CHIP, self.near)
-
-        def fwd_l(self):
-            left = lax.rem(chip + 3, 4)
-            pb, _, fb, lb = self.halves[1]
-            self.far_down.wait()
             self.put(1, left, self.total(1, left) + fb[...].astype(F32))
             send(pb.at[core, left], lb.at[1], chip_l, CHIP, self.near)
 
@@ -507,164 +485,118 @@
         copy.wait()
     pl.semaphore_wait(barrier, len(peers))
 
-    gq.go(0,0)
-    gq.go(1,0)
+    ga.go(0)
+    wd.start_a()
     pn.start()
-    gq.go(1,1)
-    gq.go(0,1)
+    ga.go(1)
     pg.start()
-    wd.start_a()
-    ga.go(0,0)
-    ga.go(1,0)
+    gq.go(0)
+    gq.go(1)
     wd.start_b()
-    gq.go(0,0)
-    gq.go(1,0)
+    ga.go(0)
+    wd.fwd()
     pn.forward()
+    gq.go(0)
     pg.forward()
-    gq.go(1,1)
-    gq.go(0,1)
-    ga.go(0,1)
-    ga.go(1,1)
-    wd.fwd_l()
-    wd.fwd_r()
+    wu.start_a()
+    gq.go(1)
+    ga.go(1)
     tn()
-    gq.go(0,0)
-    gq.go(1,0)
-    gq.go(0,1)
-    gq.go(1,1)
-    wd.sh_l()
-    wd.sh_r()
-    ga.go(0,0)
-    ga.go(1,0)
-    wu.start_a()
-    gq.go(0,0)
-    ga.go(1,1)
-    wd.far_l()
-    wd.far_r()
-    ga.go(0,1)
+    wd.sh()
     wu.start_b()
-    gq.go(1,1)
+    gq.go(0)
+    gq.go(1)
+    wd.far()
+    ga.go(0)
     rr[0].start()
     rr[1].start()
+    wq.start_a()
+    wu.fwd()
+    rr[3].start()
     rr[2].start()
-    wq.start_a()
-    ga.go(0,0)
-    ga.go(1,0)
-    wu.fwd_r()
-    wu.fwd_l()
-    rr[3].start()
+    ga.go(1)
+    gq.go(0)
+    gq.go(1)
+    wu.sh()
+    rr[0].go()
+    rr[2].go()
+    wq.start_b()
+    wq.fwd()
+    ga.go(0)
+    ga.go(1)
     rq.start()
-    rr[0].up()
-    rr[0].down()
-    rr[1].up()
-    rr[1].down()
-    wu.sh_r()
-    rr[2].up()
-    rr[2].down()
-    wu.sh_l()
+    wu.far()
+    rr[0].go()
+    rr[1].go()
+    rr[2].go()
     rq.chips()
-    wq.fwd_r()
-    wq.fwd_l()
-    ga.go(0,1)
-    ga.go(1,1)
-    rr[3].up()
-    rr[3].down()
-    rr[0].up()
-    rr[0].down()
-    rr[1].up()
-    rr[1].down()
-    wu.far_r()
-    wu.far_l()
-    rr[2].up()
-    rr[2].down()
-    rq.fwd_r()
-    rq.fwd_l()
-    ga.go(0,0)
-    ga.go(1,1)
-    rr[3].up()
-    rr[3].down()
-    rr[0].up()
-    rr[0].down()
-    rr[1].up()
-    rr[1].down()
-    rr[2].up()
-    rr[2].down()
-    wq.start_b()
-    wq.far_r()
-    wq.far_l()
+    wq.sh()
+    rr[3].go()
     rd.start()
-    rq.finish()
+    rr[0].go()
+    wq.far()
+    rr[1].go()
+    rr[2].go()
+    rd.chips()
+    rq.fwd()
+    rr[3].go()
     rr[0].finish()
     gp[0].start()
-    rr[3].up()
-    rr[3].down()
+    input_qkv()
+    rr[1].go()
+    rr[2].finish()
+    gp[2].start()
+    rr[3].go()
+    gp[0].go()
     rr[1].finish()
     gp[1].start()
-    rd.chips()
-    rr[2].finish()
-    gp[2].start()
-    wq.sh_r()
-    wq.sh_l()
-    gp[0].up()
-    gp[0].down()
+    rd.fwd()
+    gp[2].go()
     rr[3].finish()
     gp[3].start()
-    input_qkv()
-    gp[1].up()
-    gp[1].down()
-    gp[2].up()
-    gp[2].down()
-    gp[0].up()
-    gp[0].down()
-    gp[3].up()
-    gp[3].down()
-    rd.fwd_r()
-    rd.fwd_l()
-    gp[1].up()
-    gp[1].down()
-    gp[2].up()
-    gp[2].down()
-    gp[0].up()
-    gp[0].down()
-    gp[3].up()
-    gp[3].down()
-    gp[1].up()
-    gp[1].down()
-    gp[2].up()
-    gp[2].down()
+    gp[0].go()
+    gp[1].go()
+    gp[2].go()
+    rq.finish()
+    gp[3].go()
+    gp[0].go()
+    gp[1].go()
+    gp[2].go()
+    rd.finish()
+    gp[3].go()
     ru[0].start()
-    rd.finish()
     input_up(0)
-    gp[3].up()
-    gp[3].down()
+    gp[1].go()
+    ru[2].start()
+    ru[0].chips()
+    gp[3].go()
+    ru[2].chips()
     ru[1].start()
-    ru[0].chips()
-    ru[2].start()
     input_up(1)
-    ru[1].chips()
-    ru[3].start()
-    ru[2].chips()
     input_up(2)
     input_up(3)
     plane_start()
+    ru[0].fwd()
+    ru[1].chips()
+    ru[3].start()
+    ru[2].fwd()
     ru[3].chips()
-    ru[0].fwd_r()
-    ru[0].fwd_l()
-    ru[1].fwd_r()
-    ru[1].fwd_l()
-    ru[2].fwd_r()
-    ru[2].fwd_l()
-    ru[3].fwd_r()
-    ru[3].fwd_l()
+    ru[0].finish()
+    ru[1].fwd()
     plane_forward()
-    ru[0].finish()
+    ru[2].finish()
+    ru[3].fwd()
     ru[1].finish()
-    ru[2].finish()
+    plane_finish()
     ru[3].finish()
-    plane_finish()
-    assert len(landings) <= COPIES
+    assert len(landings) == COPIES
     for link in range(LINKS):
         wait_bytes(sent[link], send_sems.at[link])
+
+
+def hand_over(*refs):
+    for result, out in zip(refs[:4], refs[4:]):
+        out[...] = result[...]
 
 
 def reduce_scratch(rows, width, *lead):
@@ -678,7 +610,7 @@
 
 def shards(normed, grad_out, grad_qkv_out, pre_act, w_qkv, w_up, w_down):
     ins, outs = (normed, grad_out, grad_qkv_out, pre_act, w_qkv, w_up, w_down), (normed, w_qkv, w_up, w_down)
-    return pl.pallas_call(
+    results = pl.pallas_call(
         kernel,
         out_shape=[pltpu.VMEM(o.shape, BF) for o in outs],
         in_specs=[pl.BlockSpec(memory_space=pltpu.HBM)] * 7,
@@ -716,6 +648,13 @@
             collective_id=0, has_side_effects=True, vmem_limit_bytes=48 << 20
         ),
     )(*[pltpu.with_memory_space_constraint(a, pltpu.HBM) for a in ins])
+    return pl.pallas_call(
+        hand_over,
+        out_shape=[jax.ShapeDtypeStruct(o.shape, BF) for o in outs],
+        in_specs=[pl.BlockSpec(memory_space=pltpu.VMEM)] * 4,
+        out_specs=[pl.BlockSpec(memory_space=pltpu.VMEM)] * 4,
+        compiler_params=pltpu.CompilerParams(vmem_limit_bytes=4 << 20),
+    )(*[pltpu.with_memory_space_constraint(r, pltpu.VMEM) for r in results])
 
 
 def solution(mesh):

time: 89.3 us -> 86.5 us (0.969)
  local copies, waits for them, and re-layouts: 2.59 us -> 0 us
    unnamed x4 -> x0, local copies, waits for them, and re-layouts: 2.59 us -> none
    pallas_call x1, Pallas kernels: 85.5 us -> 84.6 us  [shards(): pl.pallas_call(kernel, out_shape=[pltpu.VMEM(o.shape, BF) for o in outs],...]
where the time goes in v4:
time: 86.5 us; the launch traced here: 86 us
  Pallas kernels  85.4 us (99%)
    pallas_call x1, Pallas kernels, shards(): pl.pallas_call(kernel, out_shape=[pltpu.VMEM(o.shape, BF) for o in outs],...  84.6 us

profile of v4, /device:TPU:1, one launch (start us, length us, event | category | flops | bytes accessed | tf_op | source)
XLA Modules:
  0.0 86.0 jit_solution(14981489493652423454)
XLA Ops:
  0.6 84.6 %shard_map.102 = (bf16[64,384]{1,0:T(8,128)(2,1)S(1)}, bf16[48,1152]{1,0:T(8,128)(2,1)S(1)}, bf16[48,1536]{1,0:T(8,128)(2,1)S(1)}, bf16[192,384]{1,0:T(8,128)(2,1)S(1)}) custom-call(bf16[64,384]{1,0:T(8,128)(2,1)} %n_in.1, bf16[64,384]{1,0:T(8,128)(2,1)} %g_in.1, bf16[64,1152]{1,0:T(8,128)(2,1)} %q_in.1, bf16[64,1536]{1,0:T(8,128)(2,1)} %p_in.1, ...), custom_call_target="tpu_custom_call" | custom-call | tf_op jit(solution)/shard_map/pallas_call | solution.py:613
  85.2 0.8 shard_map.103

commit v5 on v4

--- a/solution.py
+++ b/solution.py
@@ -80,7 +80,7 @@
     loads = []
 
     def load(src, dst):
-        copy = pltpu.make_async_copy(src, dst, load_sems.at[len(loads)])
+        copy = pltpu.make_async_copy(src, dst, load_sems.at[min(len(loads), 1)])
         copy.start()
         loads.append(copy)
         return copy
@@ -481,8 +481,6 @@
     load(wq_in, w_qkv.at[rows_of(gx, 48)])
     load_pre.wait()
     gelu()
-    for copy in loads[1:]:
-        copy.wait()
     pl.semaphore_wait(barrier, len(peers))
 
     ga.go(0)
@@ -493,6 +491,8 @@
     gq.go(0)
     gq.go(1)
     wd.start_b()
+    own = (q_in, g_in, wd_in, n_in, wu_in, wq_in)
+    wait_bytes(sum(2 * math.prod(ref.shape) for ref in own), load_sems.at[1])
     ga.go(0)
     wd.fwd()
     pn.forward()
@@ -642,7 +642,7 @@
             pltpu.VMEM((24 << 10, 128), BF),
             pltpu.SemaphoreType.DMA((LINKS,)),
             pltpu.SemaphoreType.DMA((COPIES,)),
-            pltpu.SemaphoreType.DMA((7,)),
+            pltpu.SemaphoreType.DMA((2,)),
         ],
         compiler_params=pltpu.CompilerParams(
             collective_id=0, has_side_effects=True, vmem_limit_bytes=48 << 20

time: 86.5 us -> 86.5 us (level)
  no operation moved by 1% of the time
where the time goes in v5:
time: 86.5 us; the launch traced here: 86 us
  Pallas kernels  85.3 us (99%)
    pallas_call x1, Pallas kernels, shards(): pl.pallas_call(kernel, out_shape=[pltpu.VMEM(o.shape, BF) for o in outs],...  84.5 us

profile of v5, /device:TPU:1, one launch (start us, length us, event | category | flops | bytes accessed | tf_op | source)
XLA Modules:
  0.0 86.0 jit_solution(15711503929459193237)
XLA Ops:
  0.6 84.5 %shard_map.102 = (bf16[64,384]{1,0:T(8,128)(2,1)S(1)}, bf16[48,1152]{1,0:T(8,128)(2,1)S(1)}, bf16[48,1536]{1,0:T(8,128)(2,1)S(1)}, bf16[192,384]{1,0:T(8,128)(2,1)S(1)}) custom-call(bf16[64,384]{1,0:T(8,128)(2,1)} %n_in.1, bf16[64,384]{1,0:T(8,128)(2,1)} %g_in.1, bf16[64,1152]{1,0:T(8,128)(2,1)} %q_in.1, bf16[64,1536]{1,0:T(8,128)(2,1)} %p_in.1, ...), custom_call_target="tpu_custom_call" | custom-call | tf_op jit(solution)/shard_map/pallas_call | solution.py:613
  85.2 0.8 shard_map.103
